TPU v7x, 32 devices: a whole 2x2x4 slice. The times are simulated.
32 devices in a mesh: seq: 4 (over x, core), batch: 8 (over z, y).
Axes of the slice: x: 2, y: 2, z: 4, core: 2. Of those that a mesh axis runs over, the one named last changes fastest.
Arguments:
- hidden: bfloat16 [4096, 512], P(('batch', 'seq')), parts along dimension 0, may hold values from -500 to 500
- norm_gain: float32 [512], replicated, may hold values from 0.5 to 1.5
- input_weight: bfloat16 [512, 2176], replicated, may hold values from -0.25 to 0.25
- step_weight: bfloat16 [512, 16], replicated, may hold values from -1 to 1
- conv_weight: float32 [4, 1152], replicated, may hold values from -3 to 3
- conv_bias: float32 [1152], replicated, may hold values from -3 to 3
- step_bias: float32 [16], replicated, may hold values from -11 to 1
- log_rate: float32 [16], replicated, may hold values from -3 to 6
- skip_gain: float32 [16], replicated, may hold values from 0.5 to 1.5
- gate_gain: float32 [1024], replicated, may hold values from 0.5 to 1.5
- output_weight: bfloat16 [1024, 512], replicated, may hold values from -0.1875 to 0.1875
Outputs:
- mixed: bfloat16 [4096, 512], P(('batch', 'seq')), parts along dimension 0
There are 8 independent parts, one for each index of `batch`. A program takes and returns all parts, laid end to end along the dimension named above; an argument that names none is the same for every part. Nothing has to cross between parts.
All inputs are finite; a program needn't handle non-finite values.
Results may differ from a plain program's by a relative error of at most 0.0078.
Values may be sent and summed in bfloat16 or wider, within the bound.
No kernel may reach another device: no remote copies, remote signals or barrier semaphores. Data moves between devices by JAX's collectives and lax.ppermute only.
A program may use at most 128 MiB of HBM per device.

v0:
```python
import functools

import jax
import jax.numpy as jnp
from jax import lax
from jax.experimental import pallas as pl
from jax.experimental.pallas import tpu as pltpu
from jax.sharding import PartitionSpec as P

EMBED = 512
E = 1024
N = 64
K = 4
BLOCK = 128
HEADS = 16
MIXED = E + 2 * N
TILES = MIXED // 128
PAIRS = E // 128
GROUPS = EMBED // 128
PAD = 8
EDGE = 16
eps = 1e-05
F32 = jnp.float32
BF16 = jnp.bfloat16


def dot(a, b):
    return jnp.dot(a, b, preferred_element_type=F32)


def iota(shape, axis):
    return lax.broadcasted_iota(jnp.int32, shape, axis)


def reversal():
    return (iota((128, 128), 0) + iota((128, 128), 1) == 127).astype(BF16)


def split(values, terms):
    parts = []
    for _ in range(terms):
        part = values.astype(BF16)
        parts.append(part)
        values = values - part.astype(F32)
    return parts


def exact_dot(mask, values):
    return sum(dot(mask, part) for part in split(values, 3))


def flip_lanes(rows, swap):
    return jnp.concatenate(
        [dot(rows[:, 128 * (GROUPS - 1 - g) : 128 * (GROUPS - g)], swap) for g in range(GROUPS)],
        axis=1,
    )


def both_normed(rows, gain, swap):
    floats = rows.astype(F32)
    scale = lax.rsqrt(jnp.mean(floats * floats, axis=-1, keepdims=True) + eps)
    flipped = flip_lanes(rows.astype(BF16), swap)
    return [(floats * scale * gain).astype(BF16), (flipped * scale * gain).astype(BF16)]


def half_silu(half):
    return half + half * jnp.tanh(half)


def log_decays(step_raw, step_bias, log_rate):
    v = step_raw + step_bias
    return -jnp.exp(log_rate) * (jnp.maximum(v, 0.0) + jnp.log1p(jnp.exp(-jnp.abs(v))))


def pad_lanes(values):
    return jnp.concatenate(
        [values, jnp.zeros((values.shape[0], 128 - values.shape[1]), F32)], axis=1
    )


def spread_pair(values, pair):
    index = 2 * pair + (iota(values.shape, 1) >= N).astype(jnp.int32)
    return jnp.take_along_axis(values, index, axis=1)


def own_kernel(
    x_ref,
    norm_gain_ref,
    input_weight_ref,
    step_weight_ref,
    conv_weight_ref,
    conv_bias_ref,
    step_bias_ref,
    log_rate_ref,
    activated_ref,
    edge_ref,
    silu_gate_ref,
    decay_ref,
    lift_ref,
    extended_ref,
):
    swap = reversal()
    normal = jnp.concatenate(both_normed(x_ref[...], norm_gain_ref[...], swap), axis=0)

    step_raw = dot(normal, step_weight_ref[...])
    log_decay = log_decays(step_raw, step_bias_ref[...], log_rate_ref[...])
    row, column = iota((2 * BLOCK, 2 * BLOCK), 0), iota((2 * BLOCK, 2 * BLOCK), 1)
    same = (row >= BLOCK) == (column >= BLOCK)
    before = exact_dot((same & (column <= row)).astype(BF16), log_decay)
    after = exact_dot((same & (column >= row)).astype(BF16), log_decay)

    for start in range(0, E, 256):
        gate = dot(normal, input_weight_ref[:, start : start + 256]).astype(BF16).astype(F32)
        gate = half_silu(0.5 * gate)
        for flip in range(2):
            silu_gate_ref[flip, :, start : start + 256] = gate[flip * BLOCK : (flip + 1) * BLOCK]

    for flip in range(2):
        for tile in range(TILES):
            extended_ref[flip, tile, :PAD] = jnp.zeros((PAD, 128), F32)
            extended_ref[flip, tile, PAD + BLOCK :] = jnp.zeros((PAD, 128), F32)
    for start in range(0, MIXED, 256):
        stop = min(start + 256, MIXED)
        mixed = dot(normal, input_weight_ref[:, E + start : E + stop]).astype(BF16).astype(F32)
        for flip in range(2):
            rows = mixed[flip * BLOCK : (flip + 1) * BLOCK]
            edge_ref[flip, :EDGE, start:stop] = rows[:EDGE]
            edge_ref[flip, EDGE:, start:stop] = rows[BLOCK - EDGE :]
            for tile in range(start // 128, stop // 128):
                low = tile * 128 - start
                extended_ref[flip, tile, PAD : PAD + BLOCK] = rows[:, low : low + 128]

    taps, bias = 0.5 * conv_weight_ref[...], 0.5 * conv_bias_ref[...]
    for flip in range(2):
        for tile in range(TILES):
            lanes = slice(tile * 128, tile * 128 + 128)
            ahead = bias[:, lanes]
            behind = bias[:, lanes]
            for k in range(K):
                tap = taps[k : k + 1, lanes]
                low = PAD - (K - 1) + k
                ahead = ahead + tap * extended_ref[flip, tile, low : low + BLOCK]
                low = PAD + (K - 1) - k
                behind = behind + tap * extended_ref[flip, tile, low : low + BLOCK]
            activated_ref[2 * flip, :, lanes] = half_silu(ahead).astype(BF16)
            activated_ref[2 * flip + 1, :, lanes] = half_silu(behind).astype(BF16)

    lower = iota((BLOCK, BLOCK), 0) >= iota((BLOCK, BLOCK), 1)
    for flip in range(2):
        rows = slice(flip * BLOCK, (flip + 1) * BLOCK)
        from_start, to_end = before[rows], after[rows]
        from_start_t, to_end_t = pad_lanes(from_start).T, pad_lanes(to_end).T
        for head in range(HEADS):
            at = slice(head, head + 1)
            spread = jnp.where(
                lower,
                from_start[:, at] - from_start_t[at],
                to_end[:, at] - to_end_t[at],
            )
            decay_ref[flip, head] = jnp.exp(spread)
        wide = pad_lanes(from_start), pad_lanes(to_end)
        for pair in range(PAIRS):
            lanes = slice(pair * 128, pair * 128 + 128)
            for way in range(2):
                lift_ref[2 * flip + way, :, lanes] = jnp.exp(spread_pair(wide[way], pair))


def join_kernel(count, *refs):
    received = refs[: count - 1]
    (
        norm_gain_ref,
        input_weight_ref,
        step_weight_ref,
        conv_weight_ref,
        conv_bias_ref,
        step_bias_ref,
        log_rate_ref,
        skip_gain_ref,
        gate_gain_ref,
        output_weight_ref,
        activated_ref,
        edge_ref,
        silu_gate_ref,
        decay_ref,
        lift_ref,
        out_ref,
        stack_ref,
        normal_ref,
        extended_ref,
        halo_ref,
        memory_ref,
        window_ref,
        gated_ref,
    ) = refs[count - 1 :]
    index = lax.axis_index("seq")
    swap = reversal()
    row, column = iota((BLOCK, BLOCK), 0), iota((BLOCK, BLOCK), 1)
    lower, upper = row >= column, row <= column
    taps, bias = 0.5 * conv_weight_ref[...], 0.5 * conv_bias_ref[...]
    left = iota((BLOCK, 128), 1) < N

    for offset in range(1, count):
        stack_ref[offset - 1] = received[offset - 1][...]
    halo_ref[0] = jnp.zeros(halo_ref.shape[1:], F32)
    memory_ref[...] = jnp.zeros(memory_ref.shape, F32)

    def remote(slots):
        for place, slot in enumerate(slots):
            earlier = slot < index
            offset = jnp.where(earlier, index - slot, slot + 1)
            order = jnp.where(earlier, row, 127 - row) == column
            rows = dot(order.astype(BF16), stack_ref[offset - 1])
            for flip, part in enumerate(both_normed(rows, norm_gain_ref[...], swap)):
                normal_ref[place, flip] = part
        total = len(slots) * 2 * BLOCK
        normal = normal_ref[...].reshape(total, EMBED)

        step_raw = dot(normal, step_weight_ref[...])
        log_decay = log_decays(step_raw, step_bias_ref[...], log_rate_ref[...])
        tails, wholes = [], []
        for part in range(2 * len(slots)):
            rows = log_decay[part * BLOCK : (part + 1) * BLOCK]
            tail = exact_dot((column > row).astype(BF16), rows)
            tails.append(pad_lanes(tail))
            wholes.append(pad_lanes(tail[:8] + rows[:8]))

        writers = [None] * (2 * len(slots))
        starts = [E] + list(range(0, E, 256))
        for start in starts:
            stop = min(start + 256, MIXED)
            mixed = dot(normal, input_weight_ref[:, E + start : E + stop])
            mixed = mixed.astype(BF16).astype(F32)
            for place, slot in enumerate(slots):
                keep = jnp.where(slot == index, 0.0, 1.0)
                for flip in range(2):
                    part = 2 * place + flip
                    rows = mixed[part * BLOCK : (part + 1) * BLOCK]
                    acted = []
                    for tile in range(start // 128, stop // 128):
                        low = tile * 128 - start
                        lanes = slice(tile * 128, tile * 128 + 128)
                        extended_ref[part, tile, :PAD] = keep * halo_ref[slot, flip, :, lanes]
                        extended_ref[part, tile, PAD:] = rows[:, low : low + 128]
                        halo_ref[slot + 1, flip, :, lanes] = rows[BLOCK - PAD :, low : low + 128]
                        filtered = bias[:, lanes]
                        for k in range(K):
                            at = PAD - (K - 1) + k
                            filtered = filtered + taps[k : k + 1, lanes] * extended_ref[
                                part, tile, at : at + BLOCK
                            ]
                        acted.append(half_silu(filtered).astype(BF16))
                    if start == E:
                        writers[part] = acted[0][:, :N].T
                        continue
                    decayed, scales = [], []
                    for near, values in enumerate(acted):
                        pair = start // 128 + near
                        scale = jnp.exp(spread_pair(tails[part], pair))
                        decayed.append((scale * values.astype(F32)).astype(BF16))
                        scales.append(jnp.exp(spread_pair(wholes[part], pair))[:1])
                    added = dot(writers[part], jnp.concatenate(decayed, axis=1))
                    side = jnp.where(slot < index, 0, 1)
                    lanes = slice(start, stop)
                    memory_ref[2 * flip + side, :, lanes] = (
                        jnp.concatenate(scales, axis=1) * memory_ref[2 * flip + side, :, lanes]
                        + added
                    )

    if count <= 5:
        if count > 1:
            remote(list(range(count - 1)))
    else:

        @pl.loop(0, count - 1)
        def _(slot):
            remote([slot])

    skip = exact_dot_row(skip_gain_ref[...])
    for flip in range(2):
        for way in range(2):
            chain = 2 * flip + way
            if way == 0:
                window_ref[:PAD] = halo_ref[index, flip]
                window_ref[PAD : PAD + EDGE] = edge_ref[flip, :EDGE]
            else:
                keep = jnp.where(index < count - 1, 1.0, 0.0)
                window_ref[PAD - 8 : PAD - 8 + EDGE] = edge_ref[flip, EDGE:]
                for step in range(K - 1):
                    window_ref[EDGE + step : EDGE + step + 1] = (
                        keep * halo_ref[count - 1, flip, PAD - 1 - step : PAD - step]
                    )
            filtered = bias
            for k in range(K):
                at = PAD - (K - 1) + k if way == 0 else (K - 1) - k
                filtered = filtered + taps[k : k + 1] * window_ref[at : at + EDGE]
            patch = half_silu(filtered).astype(BF16)

            def acted(tile):
                lanes = slice(tile * 128, tile * 128 + 128)
                if way == 0:
                    parts = [patch[:, lanes], activated_ref[chain, EDGE:, lanes]]
                else:
                    parts = [activated_ref[chain, : BLOCK - EDGE, lanes], patch[:, lanes]]
                return jnp.concatenate(parts, axis=0)

            maps = acted(PAIRS)
            writer, reader = maps[:, :N], maps[:, N:]
            scores = lax.dot_general(
                reader, writer, (((1,), (1,)), ((), ())), preferred_element_type=F32
            )
            scores = jnp.where(lower if way == 0 else upper, scores, 0.0)
            squares = jnp.zeros((BLOCK, 128), F32)
            doubled = jnp.concatenate([reader, reader], axis=1)
            for pair in range(PAIRS):
                lanes = slice(pair * 128, pair * 128 + 128)
                signal = acted(pair)
                zeros = jnp.zeros_like(signal)
                signals = jnp.concatenate(
                    [jnp.where(left, signal, zeros), jnp.where(left, zeros, signal)], axis=0
                )
                weights = jnp.concatenate(
                    [
                        (decay_ref[flip, 2 * pair + near] * scores).astype(BF16)
                        for near in range(2)
                    ],
                    axis=1,
                )
                inside = dot(weights, signals)
                memory = jnp.concatenate(split(memory_ref[chain, :, lanes], 2), axis=0)
                carried = dot(doubled, memory)
                inside = inside + lift_ref[chain, :, lanes] * carried
                gated = inside + skip[:, lanes] * signal.astype(F32)
                gated = gated * silu_gate_ref[flip, :, lanes]
                squares = squares + gated * gated
                gated_ref[chain, :, lanes] = gated
            scale = lax.rsqrt(jnp.sum(squares, axis=1, keepdims=True) * (1.0 / E) + eps)
            for pair in range(PAIRS):
                lanes = slice(pair * 128, pair * 128 + 128)
                gated_ref[chain, :, lanes] = (
                    gated_ref[chain, :, lanes] * scale * gate_gain_ref[:, lanes]
                )

    normed = gated_ref[...].astype(BF16).reshape(4 * BLOCK, E)
    made = dot(normed, output_weight_ref[...])
    straight, turned = made[: 2 * BLOCK], made[2 * BLOCK :]
    high, low = split(turned, 2)
    both = straight + flip_lanes(high, swap) + flip_lanes(low, swap)
    backward = both[BLOCK:].astype(BF16).astype(F32)
    out_ref[...] = (both[:BLOCK] + backward).astype(BF16)


def exact_dot_row(row):
    select = (iota((HEADS, E), 1) // N == iota((HEADS, E), 0)).astype(BF16)
    rows = jnp.broadcast_to(row, (8, HEADS))
    return sum(dot(part, select) for part in split(rows, 3))[:1]


def on_device(
    hidden,
    norm_gain,
    input_weight,
    step_weight,
    conv_weight,
    conv_bias,
    step_bias,
    log_rate,
    skip_gain,
    gate_gain,
    output_weight,
):
    count = lax.axis_size("seq")
    received = [
        lax.ppermute(hidden, "seq", [(i, (i + offset) % count) for i in range(count)])
        for offset in range(1, count)
    ]
    row = lambda vector: vector.reshape(1, -1)
    whole = pl.BlockSpec(memory_space=pltpu.VMEM)
    shared = [
        row(norm_gain),
        input_weight,
        step_weight,
        conv_weight,
        row(conv_bias),
        row(step_bias),
        row(log_rate),
    ]
    shape = jax.ShapeDtypeStruct
    own = pl.pallas_call(
        own_kernel,
        out_shape=[
            shape((4, BLOCK, MIXED), BF16),
            shape((2, 2 * EDGE, MIXED), F32),
            shape((2, BLOCK, E), F32),
            shape((2, HEADS, BLOCK, BLOCK), F32),
            shape((4, BLOCK, E), F32),
        ],
        in_specs=[whole] * 8,
        out_specs=[whole] * 5,
        scratch_shapes=[pltpu.VMEM((2, TILES, BLOCK + 2 * PAD, 128), F32)],
        compiler_params=pltpu.CompilerParams(vmem_limit_bytes=24 * 2**20),
        cost_estimate=pl.CostEstimate(
            flops=10**9, bytes_accessed=10**7, transcendentals=10**6
        ),
        name="own_block",
    )(hidden, *shared)
    together = count - 1 if count <= 5 else 1
    return pl.pallas_call(
        functools.partial(join_kernel, count),
        out_shape=shape((BLOCK, EMBED), BF16),
        in_specs=[whole] * (count - 1 + 10 + 5),
        out_specs=whole,
        scratch_shapes=[
            pltpu.VMEM((max(count - 1, 1), BLOCK, EMBED), BF16),
            pltpu.VMEM((max(together, 1), 2, BLOCK, EMBED), BF16),
            pltpu.VMEM((2 * max(together, 1), TILES, PAD + BLOCK, 128), F32),
            pltpu.VMEM((count, 2, PAD, MIXED), F32),
            pltpu.VMEM((4, N, E), F32),
            pltpu.VMEM((PAD + EDGE, MIXED), F32),
            pltpu.VMEM((4, BLOCK, E), F32),
        ],
        compiler_params=pltpu.CompilerParams(vmem_limit_bytes=32 * 2**20),
        cost_estimate=pl.CostEstimate(
            flops=2 * 10**9, bytes_accessed=10**7, transcendentals=10**6
        ),
        name="join_blocks",
    )(
        *received,
        *shared,
        row(skip_gain),
        row(gate_gain),
        output_weight,
        *own,
    )


def solution(mesh):
    in_specs = (P(("batch", "seq"), None), P(), P(), P(), P(), P(), P(), P(), P(), P(), P())
    out_specs = P(("batch", "seq"), None)
    return jax.shard_map(
        on_device, mesh=mesh, in_specs=in_specs, out_specs=out_specs, check_vma=False
    )
```

profile of v0, /device:TPU:0, one launch (start us, length us, event | category | flops | bytes accessed | tf_op | source)
XLA Modules:
  0.0 23.6 jit_solution(15380403063613125251)
XLA Ops:
  0.0 0.0 copy-start.4
  0.0 0.0 copy-start.9
  0.0 0.0 copy-start.7
  0.0 0.0 copy-start.5
  0.0 0.0 copy-start.11
  0.0 3.0 %collective-permute-start.1 = (bf16[128,512]{1,0:T(8,128)(2,1)}, bf16[128,512]{1,0:T(8,128)(2,1)S(1)}, u32[]{:S(2)}, u32[]{:S(2)}) collective-permute-start(bf16[128,512]{1,0:T(8,128)(2,1)} %x_ref.1), channel_id=1, source_target_pairs={{0,16},{8,24},{16,0},{24,8},{1,17},{9,25},{17,1},{25,9},{2,18},{10... | collective-permute-start | bytes 393224 | tf_op jit(solution)/shard_map/ppermute | solution.py:373
  3.0 0.0 collective-permute-start
  3.0 1.7 %collective-permute-start.2 = (bf16[128,512]{1,0:T(8,128)(2,1)}, bf16[128,512]{1,0:T(8,128)(2,1)S(1)}, u32[]{:S(2)}, u32[]{:S(2)}) collective-permute-start(bf16[128,512]{1,0:T(8,128)(2,1)} %x_ref.1), channel_id=1, source_target_pairs={{0,24},{8,0},{16,8},{24,16},{1,25},{9,1},{17,9},{25,17},{2,26},{10... | collective-permute-start | bytes 393224 | tf_op jit(solution)/shard_map/ppermute | solution.py:373
  4.8 0.7 %reshape.19.conv_bias_ref.refs_7_ = f32[1,1152]{1,0:T(1,128)S(1)} reshape(f32[1152]{0:T(1024)} %param.16) | data formatting | bytes 9216 | tf_op jit(solution)/shard_map/reshape | solution.py:376
  5.5 0.8 %copy.13.step_weight_ref.refs_5_ = bf16[512,16]{1,0:T(8,128)(2,1)S(1)} copy(bf16[512,16]{0,1:T(8,128)(2,1)} %param.14) | data formatting | bytes 32768 | tf_op args[3]
  6.3 0.0 copy-start
  6.3 1.6 %copy-done = bf16[512,2176]{1,0:T(8,128)(2,1)S(1)} copy-done((bf16[512,2176]{1,0:T(8,128)(2,1)S(1)}, bf16[512,2176]{1,0:T(8,128)(2,1)}, u32[]{:S(2)}) %copy-start) | copy-done | bytes 2228248
  8.0 0.0 copy-start.3
  8.0 0.7 %copy-done.3 = f32[4,1152]{1,0:T(4,128)S(1)} copy-done((f32[4,1152]{1,0:T(4,128)S(1)}, f32[4,1152]{1,0:T(4,128)}, u32[]{:S(2)}) %copy-start.3) | copy-done | bytes 18456
  8.7 0.0 copy-start.6
  8.7 0.7 %copy-done.6 = f32[512]{0:T(512)S(1)} copy-done((f32[512]{0:T(512)S(1)}, f32[512]{0:T(512)}, u32[]{:S(2)}) %copy-start.6) | copy-done | bytes 2072
  9.4 0.0 copy-start.8
  9.4 0.7 %copy-done.8 = f32[16]{0:T(128)S(1)} copy-done((f32[16]{0:T(128)S(1)}, f32[16]{0:T(128)}, u32[]{:S(2)}) %copy-start.8) | copy-done | bytes 88
  10.0 0.0 copy-start.10
  10.0 0.7 %copy-done.10 = f32[16]{0:T(128)S(1)} copy-done((f32[16]{0:T(128)S(1)}, f32[16]{0:T(128)}, u32[]{:S(2)}) %copy-start.10) | copy-done | bytes 88
  10.7 0.0 copy-start.12
  10.7 0.9 %copy-done.12 = bf16[128,512]{1,0:T(8,128)(2,1)S(1)} copy-done((bf16[128,512]{1,0:T(8,128)(2,1)S(1)}, bf16[128,512]{1,0:T(8,128)(2,1)}, u32[]{:S(2)}) %copy-start.12) | copy-done | bytes 131096
  11.6 0.0 copy-start.1
  11.6 0.0 copy-start.2
  11.6 3.6 %own_block.1 = (bf16[4,128,1152]{2,1,0:T(8,128)(2,1)S(1)}, f32[2,32,1152]{2,1,0:T(8,128)S(1)}, f32[2,128,1024]{2,1,0:T(8,128)S(1)}, f32[2,16,128,128]{3,2,1,0:T(8,128)S(1)}, f32[4,128,1024]{2,1,0:T(8,128)S(1)}) custom-call(bf16[128,512]{1,0:T(8,128)(2,1)S(1)} %copy-done.12, f32[1,512]{1,0:T(1,128)S(1)} %bitcast.6, bf16[512,2176]{1,0:T(8,128)(2,1)S(1)} %copy-done, ...), custom_call_target="tpu_custom_call" | custom-call | flops 1000000000 | bytes 10000000 | tf_op jit(solution)/shard_map/own_block/pallas_call | solution.py:388
  15.2 0.0 collective-permute-done.1.refs_1_
  15.2 0.0 collective-permute-done.refs_0_
  15.2 0.0 collective-permute-done.2.refs_2_
  15.3 0.0 copy-done.4
  15.3 0.0 copy-done.9
  15.3 0.0 copy-done.7
  15.3 0.0 copy-done.5
  15.3 0.0 copy-done.11
  15.3 0.0 copy-done.1
  15.3 0.0 copy-done.2
  15.3 8.3 %join_blocks.1 = bf16[128,512]{1,0:T(8,128)(2,1)} custom-call(bf16[128,512]{1,0:T(8,128)(2,1)S(1)} %collective-permute-done.refs_0_, bf16[128,512]{1,0:T(8,128)(2,1)S(1)} %collective-permute-done.1.refs_1_, bf16[128,512]{1,0:T(8,128)(2,1)S(1)} %collective-permute-done.2.refs_2_, f32[1,512]{1,0:T(1,128)S(1)} %bitcast.7, bf16[512,2176]{1,0:T(8,128)(2,1)S(1)} %copy-done.1, ...), custom_call_target="tpu_custom_call" | custom-call | flops 2000000000 | bytes 10000000 | tf_op jit(solution)/shard_map/join_blocks/pallas_call | solution.py:407
Async XLA Ops:
  0.0 15.3 %copy-start.4 = (f32[4,1152]{1,0:T(4,128)S(1)}, f32[4,1152]{1,0:T(4,128)}, u32[]{:S(2)}) copy-start(f32[4,1152]{1,0:T(4,128)} %refs_6_.1) | copy-start | bytes 55300
  0.0 15.3 %copy-start.9 = (f32[16]{0:T(128)S(1)}, f32[16]{0:T(128)}, u32[]{:S(2)}) copy-start(f32[16]{0:T(128)} %param.17) | copy-start | bytes 196
  0.0 15.3 %copy-start.7 = (f32[512]{0:T(512)S(1)}, f32[512]{0:T(512)}, u32[]{:S(2)}) copy-start(f32[512]{0:T(512)} %param.12) | copy-start | bytes 6148
  0.0 15.3 %copy-start.5 = (f32[1024]{0:T(1024)S(1)}, f32[1024]{0:T(1024)}, u32[]{:S(2)}) copy-start(f32[1024]{0:T(1024)} %param.20) | copy-start | bytes 12292
  0.0 15.3 %copy-start.11 = (f32[16]{0:T(128)S(1)}, f32[16]{0:T(128)}, u32[]{:S(2)}) copy-start(f32[16]{0:T(128)} %param.19) | copy-start | bytes 196
  0.0 15.2 %collective-permute-start.1 = (bf16[128,512]{1,0:T(8,128)(2,1)}, bf16[128,512]{1,0:T(8,128)(2,1)S(1)}, u32[]{:S(2)}, u32[]{:S(2)}) collective-permute-start(bf16[128,512]{1,0:T(8,128)(2,1)} %x_ref.1), channel_id=1, source_target_pairs={{0,16},{8,24},{16,0},{24,8},{1,17},{9,25},{17,1},{25,9},{2,18},{10... | collective-permute-start | bytes 393224 | tf_op jit(solution)/shard_map/ppermute | solution.py:373
  3.0 12.2 %collective-permute-start = (bf16[128,512]{1,0:T(8,128)(2,1)}, bf16[128,512]{1,0:T(8,128)(2,1)S(1)}, u32[]{:S(2)}, u32[]{:S(2)}) collective-permute-start(bf16[128,512]{1,0:T(8,128)(2,1)} %x_ref.1), channel_id=1, source_target_pairs={{0,8},{8,16},{16,24},{24,0},{1,9},{9,17},{17,25},{25,1},{2,10},{10... | collective-permute-start | bytes 393224 | tf_op jit(solution)/shard_map/ppermute | solution.py:373
  3.0 12.2 %collective-permute-start.2 = (bf16[128,512]{1,0:T(8,128)(2,1)}, bf16[128,512]{1,0:T(8,128)(2,1)S(1)}, u32[]{:S(2)}, u32[]{:S(2)}) collective-permute-start(bf16[128,512]{1,0:T(8,128)(2,1)} %x_ref.1), channel_id=1, source_target_pairs={{0,24},{8,0},{16,8},{24,16},{1,25},{9,1},{17,9},{25,17},{2,26},{10... | collective-permute-start | bytes 393224 | tf_op jit(solution)/shard_map/ppermute | solution.py:373
  6.3 1.6 %copy-start = (bf16[512,2176]{1,0:T(8,128)(2,1)S(1)}, bf16[512,2176]{1,0:T(8,128)(2,1)}, u32[]{:S(2)}) copy-start(bf16[512,2176]{1,0:T(8,128)(2,1)} %refs_4_.1) | copy-start | bytes 6684676
  8.0 0.7 %copy-start.3 = (f32[4,1152]{1,0:T(4,128)S(1)}, f32[4,1152]{1,0:T(4,128)}, u32[]{:S(2)}) copy-start(f32[4,1152]{1,0:T(4,128)} %refs_6_.1) | copy-start | bytes 55300
  8.7 0.7 %copy-start.6 = (f32[512]{0:T(512)S(1)}, f32[512]{0:T(512)}, u32[]{:S(2)}) copy-start(f32[512]{0:T(512)} %param.12) | copy-start | bytes 6148
  9.4 0.7 %copy-start.8 = (f32[16]{0:T(128)S(1)}, f32[16]{0:T(128)}, u32[]{:S(2)}) copy-start(f32[16]{0:T(128)} %param.17) | copy-start | bytes 196
  10.0 0.7 %copy-start.10 = (f32[16]{0:T(128)S(1)}, f32[16]{0:T(128)}, u32[]{:S(2)}) copy-start(f32[16]{0:T(128)} %param.18) | copy-start | bytes 196
  10.7 0.9 %copy-start.12 = (bf16[128,512]{1,0:T(8,128)(2,1)S(1)}, bf16[128,512]{1,0:T(8,128)(2,1)}, u32[]{:S(2)}) copy-start(bf16[128,512]{1,0:T(8,128)(2,1)} %x_ref.1) | copy-start | bytes 393220
  11.6 3.7 %copy-start.1 = (bf16[512,2176]{1,0:T(8,128)(2,1)S(1)}, bf16[512,2176]{1,0:T(8,128)(2,1)}, u32[]{:S(2)}) copy-start(bf16[512,2176]{1,0:T(8,128)(2,1)} %refs_4_.1) | copy-start | bytes 6684676
  11.6 3.7 %copy-start.2 = (bf16[1024,512]{1,0:T(8,128)(2,1)S(1)}, bf16[1024,512]{1,0:T(8,128)(2,1)}, u32[]{:S(2)}) copy-start(bf16[1024,512]{1,0:T(8,128)(2,1)} %refs_12_.1) | copy-start | bytes 3145732
where the time goes:
time: 24 us; the launch traced here: 23.6 us
  Pallas kernels  11.9 us (50%)
  local copies, waits for them, and re-layouts  6.81 us (28%)
  starting transfers between devices  4.76 us (20%)
    pallas_call x1, Pallas kernels, on_device(): pl.pallas_call(functools.partial(join_kernel, count), out_shape=shape((BL...  8.31 us
    unnamed x27, local copies, waits for them, and re-layouts  6.11 us
    ppermute x3, starting transfers between devices, on_device(): lax.ppermute(hidden, 'seq', [(i, (i + offset) % count) for i in range(cou...  4.76 us
    pallas_call x1, Pallas kernels, on_device(): pl.pallas_call(own_kernel, out_shape=[shape((4, BLOCK, MIXED), BF16), sha...  3.63 us
    reshape x1, local copies, waits for them, and re-layouts, on_device(): row = lambda vector: vector.reshape(1, -1)  0.7 us
  transfers between devices with their start and end apart: 3, of which 0 were waited for; matrix products, arithmetic and copies ran while one was open for 7% of the time, Pallas kernels for 15%

commit v1 on v0

v1 whole, which is shorter than its diff:
```python
import functools

import jax
import jax.numpy as jnp
from jax import lax
from jax.experimental import pallas as pl
from jax.experimental.pallas import tpu as pltpu
from jax.sharding import PartitionSpec as P

EMBED = 512
E = 1024
N = 64
K = 4
BLOCK = 128
HEADS = 16
MIXED = E + 2 * N
TILES = MIXED // 128
PAIRS = E // 128
GROUPS = EMBED // 128
PAD = 8
EDGE = 16
eps = 1e-05
F32 = jnp.float32
BF16 = jnp.bfloat16


def dot(a, b):
    return jnp.dot(a, b, preferred_element_type=F32)


def dot_rows(a, b):
    return lax.dot_general(a, b, (((1,), (1,)), ((), ())), preferred_element_type=F32)


def iota(shape, axis):
    return lax.broadcasted_iota(jnp.int32, shape, axis)


def reversal():
    return (iota((128, 128), 0) + iota((128, 128), 1) == 127).astype(BF16)


def split(values, terms):
    parts = []
    for _ in range(terms):
        part = values.astype(BF16)
        parts.append(part)
        values = values - part.astype(F32)
    return parts


def exact_dot(values, mask):
    return sum(dot(part, mask) for part in split(values, 3))


def flip_lanes(rows, swap):
    return jnp.concatenate(
        [dot(rows[:, 128 * (GROUPS - 1 - g) : 128 * (GROUPS - g)], swap) for g in range(GROUPS)],
        axis=1,
    )


def both_normed(rows, gain, swap):
    floats = rows.astype(F32)
    scale = lax.rsqrt(jnp.mean(floats * floats, axis=-1, keepdims=True) + eps)
    flipped = flip_lanes(rows.astype(BF16), swap)
    return [(floats * scale * gain).astype(BF16), (flipped * scale * gain).astype(BF16)]


def half_silu(half):
    return half + half * jnp.tanh(half)


def column_of(row):
    shape = (HEADS, HEADS)
    return jnp.sum(
        jnp.where(iota(shape, 0) == iota(shape, 1), row, 0.0), axis=1, keepdims=True
    )


def log_decays(step_raw, step_bias, log_rate):
    v = step_raw + column_of(step_bias)
    u = jnp.exp(-jnp.abs(v))
    series = 1.0 / 7.0
    for order in range(6, 0, -1):
        series = 1.0 / order - u * series
    rest = jnp.where(u < 0.0625, u * series, jnp.log(1.0 + u))
    return -jnp.exp(column_of(log_rate)) * (jnp.maximum(v, 0.0) + rest)


def spread_heads(values, terms, start, stop, each):
    parts = jnp.concatenate(split(values, terms), axis=0)
    shape = (terms * HEADS, stop - start)
    head = (iota(shape, 1) + start) // each
    select = (iota(shape, 0) % HEADS == head).astype(BF16)
    return lax.dot_general(parts, select, (((0,), (0,)), ((), ())), preferred_element_type=F32)


def lanes_of(tile):
    return slice(tile * 128, tile * 128 + 128)


def chunks(width):
    return [(start, min(start + 256, width)) for start in range(0, width, 256)]


def filtered(source, at, lanes, taps, bias, backward=False, rows=BLOCK):
    result = bias[:, lanes]
    for k in range(K):
        low = at + ((K - 1) - k if backward else k - (K - 1))
        result = result + taps[k : k + 1, lanes] * source[low : low + rows]
    return result


def decay_kernel(*refs):
    sources, refs = refs[:5], refs[5:]
    (normal_ref, decay_ref, lift_ref), refs = refs[:3], refs[3:]
    held, semaphores = refs[:5], refs[5]
    copies = [
        pltpu.make_async_copy(sources[place], held[place], semaphores.at[place])
        for place in range(5)
    ]
    for copy in copies:
        copy.start()
    for copy in copies:
        copy.wait()
    x_ref, norm_gain_ref, step_weight_ref, step_bias_ref, log_rate_ref = held
    normal = jnp.concatenate(both_normed(x_ref[...], norm_gain_ref[...], reversal()), axis=0)
    normal_ref[...] = normal
    log_decay = log_decays(
        dot_rows(step_weight_ref[...], normal), step_bias_ref[...], log_rate_ref[...]
    )
    row, column = iota((BLOCK, BLOCK), 0), iota((BLOCK, BLOCK), 1)
    lower = row >= column
    both = jnp.concatenate([log_decay[:, :BLOCK], log_decay[:, BLOCK:]], axis=0)
    before = exact_dot(both, (row <= column).astype(BF16))
    after = exact_dot(both, (row >= column).astype(BF16))
    for flip in range(2):
        heads = slice(flip * HEADS, (flip + 1) * HEADS)
        for pair in range(PAIRS):
            low, high = 2 * pair * BLOCK, 2 * (pair + 1) * BLOCK
            from_start = spread_heads(before[heads], 3, low, high, BLOCK)
            to_end = spread_heads(after[heads], 3, low, high, BLOCK)
            for near in range(2):
                at = flip * HEADS + 2 * pair + near
                lanes = lanes_of(near)
                decay_ref[flip, 2 * pair + near] = jnp.exp(
                    jnp.where(
                        lower,
                        from_start[:, lanes] - before[at : at + 1],
                        to_end[:, lanes] - after[at : at + 1],
                    )
                )
        for start, stop in chunks(E):
            for way, rows in enumerate((before, after)):
                lift_ref[2 * flip + way, :, start:stop] = spread_heads(
                    jnp.exp(rows[heads]), 2, start, stop, N
                )


def own_kernel(
    normal_ref,
    input_weight_ref,
    conv_weight_ref,
    conv_bias_ref,
    activated_ref,
    edge_ref,
    silu_gate_ref,
    extended_ref,
):
    normal = normal_ref[...]
    taps, bias = 0.5 * conv_weight_ref[...], 0.5 * conv_bias_ref[...].reshape(1, MIXED)
    for start, stop in chunks(MIXED):
        mixed = dot(normal, input_weight_ref[:, E + start : E + stop]).astype(BF16).astype(F32)
        for flip in range(2):
            rows = mixed[flip * BLOCK : (flip + 1) * BLOCK]
            edge_ref[flip, :EDGE, start:stop] = rows[:EDGE]
            edge_ref[flip, EDGE:, start:stop] = rows[BLOCK - EDGE :]
            for tile in range(start // 128, stop // 128):
                lanes = lanes_of(tile)
                place = extended_ref.at[flip, tile]
                place[:PAD] = jnp.zeros((PAD, 128), F32)
                place[PAD + BLOCK :] = jnp.zeros((PAD, 128), F32)
                place[PAD : PAD + BLOCK] = rows[:, tile * 128 - start : tile * 128 - start + 128]
                for way in range(2):
                    half = filtered(place, PAD, lanes, taps, bias, way == 1)
                    activated_ref[2 * flip + way, :, lanes] = half_silu(half).astype(BF16)
    for start, stop in chunks(E):
        gate = dot(normal, input_weight_ref[:, start:stop]).astype(BF16).astype(F32)
        gate = half_silu(0.5 * gate)
        for flip in range(2):
            silu_gate_ref[flip, :, start:stop] = gate[flip * BLOCK : (flip + 1) * BLOCK]


def chain_rows(mask, index, block, gain, swap):
    row, column = iota((BLOCK, BLOCK), 0), iota((BLOCK, BLOCK), 1)
    order = jnp.where((index ^ mask) < index, row, 127 - row) == column
    return both_normed(dot(order.astype(BF16), block), gain, swap)


def ahead_kernel(
    mask,
    block_ref,
    norm_gain_ref,
    input_weight_ref,
    step_weight_ref,
    conv_weight_ref,
    conv_bias_ref,
    step_bias_ref,
    log_rate_ref,
    activated_ref,
    edge_ref,
    log_decay_ref,
    extended_ref,
):
    index = lax.axis_index("seq")
    normal = jnp.concatenate(
        chain_rows(mask, index, block_ref[...], norm_gain_ref[...], reversal()), axis=0
    )
    log_decay_ref[...] = log_decays(
        dot_rows(step_weight_ref[...], normal), step_bias_ref[...], log_rate_ref[...]
    )
    taps, bias = 0.5 * conv_weight_ref[...], 0.5 * conv_bias_ref[...].reshape(1, MIXED)
    for start, stop in chunks(MIXED):
        mixed = dot(normal, input_weight_ref[:, E + start : E + stop]).astype(BF16).astype(F32)
        for flip in range(2):
            rows = mixed[flip * BLOCK : (flip + 1) * BLOCK]
            edge_ref[flip, :EDGE, start:stop] = rows[:EDGE]
            edge_ref[flip, EDGE:, start:stop] = rows[BLOCK - PAD :]
            for tile in range(start // 128, stop // 128):
                lanes = lanes_of(tile)
                place = extended_ref.at[flip, tile]
                place[:PAD] = jnp.zeros((PAD, 128), F32)
                place[PAD:] = rows[:, tile * 128 - start : tile * 128 - start + 128]
                half = filtered(place, PAD, lanes, taps, bias)
                activated_ref[flip, :, lanes] = half_silu(half).astype(BF16)


def join_kernel(count, top, *refs):
    others = [mask for mask in range(1, count) if mask != top]
    received, refs = refs[: len(others)], refs[len(others) :]
    (
        norm_gain_ref,
        input_weight_ref,
        step_weight_ref,
        conv_weight_ref,
        conv_bias_ref,
        step_bias_ref,
        log_rate_ref,
        skip_gain_ref,
        gate_gain_ref,
        output_weight_ref,
        decay_ref,
        lift_ref,
        activated_ref,
        edge_ref,
        silu_gate_ref,
        ahead_ref,
        ahead_edge_ref,
        ahead_log_decay_ref,
        out_ref,
        normal_ref,
        extended_ref,
        halo_ref,
        memory_ref,
        window_ref,
        patch_ref,
        gated_ref,
    ) = refs
    index = lax.axis_index("seq")
    swap = reversal()
    row, column = iota((BLOCK, BLOCK), 0), iota((BLOCK, BLOCK), 1)
    lower, upper = row >= column, row <= column
    left = column < N
    taps, bias = 0.5 * conv_weight_ref[...], 0.5 * conv_bias_ref[...].reshape(1, MIXED)

    def halo_of(block, flip):
        exists = jnp.where((block >= 0) & (block < count), 1.0, 0.0)
        place = jnp.clip((block ^ index) - 1, 0, count - 2)
        return exists * halo_ref[place, flip]

    for place, mask in enumerate(others):
        block = received[place][...]
        for flip, part in enumerate(chain_rows(mask, index, block, norm_gain_ref[...], swap)):
            low = (2 * place + flip) * BLOCK
            normal_ref[low : low + BLOCK] = part
    normal = normal_ref[...]
    log_decay = log_decays(
        dot_rows(step_weight_ref[...], normal), step_bias_ref[...], log_rate_ref[...]
    )
    pieces = {}
    for flip in range(2):
        for place, mask in enumerate(others):
            low = (2 * place + flip) * BLOCK
            pieces[mask, flip] = log_decay[:, low : low + BLOCK]
        pieces[top, flip] = ahead_log_decay_ref[:, flip * BLOCK : (flip + 1) * BLOCK]
    parts = [(mask, flip) for mask in range(1, count) for flip in range(2)]
    tails = exact_dot(
        jnp.concatenate([pieces[part] for part in parts], axis=0), (row > column).astype(BF16)
    )
    wholes = {part: jnp.sum(pieces[part], axis=1, keepdims=True) for part in parts}
    faded = [[], []]
    for at, (mask, flip) in enumerate(parts):
        tail = tails[at * HEADS : (at + 1) * HEADS]
        block = index ^ mask
        for other in range(1, count):
            if other != mask:
                between = index ^ other
                later = ((block < between) & (between < index)) | (
                    (index < between) & (between < block)
                )
                tail = tail + jnp.where(later, wholes[other, flip], 0.0)
        faded[flip].append(jnp.exp(tail))
    faded = [jnp.concatenate(rows, axis=1) for rows in faded]

    for flip in range(2):
        halo_ref[top - 1, flip] = ahead_edge_ref[flip, EDGE:]
    writers = [None, None]
    order = chunks(MIXED)
    for start, stop in order[-1:] + order[:-1]:
        mixed = dot(normal, input_weight_ref[:, E + start : E + stop]).astype(BF16).astype(F32)
        for place, mask in enumerate(others):
            for flip in range(2):
                low = (2 * place + flip) * BLOCK
                halo_ref[mask - 1, flip, :, start:stop] = mixed[low + BLOCK - PAD : low + BLOCK]
        for flip in range(2):
            acted = {}
            for mask in range(1, count):
                block = index ^ mask
                before = jnp.where(block < index, block - 1, block + 1)
                halo = halo_of(before, flip)[:, start:stop]
                if mask == top:
                    near = []
                    for tile in range(start // 128, stop // 128):
                        lanes = lanes_of(tile)
                        spot = patch_ref.at[flip, tile]
                        spot[:PAD] = halo[:, tile * 128 - start : tile * 128 - start + 128]
                        spot[PAD:] = ahead_edge_ref[flip, :EDGE, lanes]
                        half = filtered(spot, PAD, lanes, taps, bias, False, EDGE)
                        patch = half_silu(half).astype(BF16)
                        near.append(
                            jnp.concatenate([patch, ahead_ref[flip, EDGE:, lanes]], axis=0)
                        )
                    acted[mask] = jnp.concatenate(near, axis=1)
                    continue
                place = others.index(mask)
                low = (2 * place + flip) * BLOCK
                near = []
                for tile in range(start // 128, stop // 128):
                    at = tile * 128 - start
                    spot = extended_ref.at[2 * place + flip, tile]
                    spot[:PAD] = halo[:, at : at + 128]
                    spot[PAD:] = mixed[low : low + BLOCK, at : at + 128]
                    half = filtered(spot, PAD, lanes_of(tile), taps, bias)
                    near.append(half_silu(half).astype(BF16))
                acted[mask] = jnp.concatenate(near, axis=1)
            if start == E:
                sides = []
                for mask in range(1, count):
                    maps = acted[mask].T[:N]
                    earlier = jnp.where((index ^ mask) < index, 1.0, 0.0).astype(BF16)
                    later = jnp.where((index ^ mask) < index, 0.0, 1.0).astype(BF16)
                    sides.append(jnp.concatenate([maps * earlier, maps * later], axis=0))
                writers[flip] = jnp.concatenate(sides, axis=1)
                continue
            fade = spread_heads(faded[flip], 2, start, stop, N)
            decayed = [
                (fade[at * BLOCK : (at + 1) * BLOCK] * acted[at + 1].astype(F32)).astype(BF16)
                for at in range(count - 1)
            ]
            memory = dot(writers[flip], jnp.concatenate(decayed, axis=0))
            for way in range(2):
                high, low = split(memory[way * N : (way + 1) * N], 2)
                memory_ref[2 * flip + way, :N, start:stop] = high
                memory_ref[2 * flip + way, N:, start:stop] = low

    skip = wide_row(skip_gain_ref[...])
    for flip in range(2):
        for way in range(2):
            chain = 2 * flip + way
            spot = window_ref.at[chain]
            if way == 0:
                spot[:PAD] = halo_of(index - 1, flip)
                spot[PAD:] = edge_ref[flip, :EDGE]
            else:
                halo = halo_of(index + 1, flip)
                spot[:EDGE] = edge_ref[flip, EDGE:]
                for step in range(K - 1):
                    spot[EDGE + step : EDGE + step + 1] = halo[PAD - 1 - step : PAD - step]
            at = PAD if way == 0 else 0
            half = filtered(spot, at, slice(0, MIXED), taps, bias, way == 1, EDGE)
            patch = half_silu(half).astype(BF16)

            def acted(tile):
                lanes = lanes_of(tile)
                if way == 0:
                    near = [patch[:, lanes], activated_ref[chain, EDGE:, lanes]]
                else:
                    near = [activated_ref[chain, : BLOCK - EDGE, lanes], patch[:, lanes]]
                return jnp.concatenate(near, axis=0)

            maps = acted(PAIRS)
            writer, reader = maps[:, :N], maps[:, N:]
            scores = jnp.where(lower if way == 0 else upper, dot_rows(reader, writer), 0.0)
            squares = jnp.zeros((BLOCK, 128), F32)
            doubled = jnp.concatenate([reader, reader], axis=1)
            for pair in range(PAIRS):
                lanes = lanes_of(pair)
                signal = acted(pair)
                zeros = jnp.zeros_like(signal)
                signals = jnp.concatenate(
                    [jnp.where(left, signal, zeros), jnp.where(left, zeros, signal)], axis=0
                )
                weights = jnp.concatenate(
                    [
                        (decay_ref[flip, 2 * pair + near] * scores).astype(BF16)
                        for near in range(2)
                    ],
                    axis=1,
                )
                inside = dot(weights, signals)
                carried = dot(doubled, memory_ref[chain, :, lanes])
                inside = inside + lift_ref[chain, :, lanes] * carried
                gated = inside + skip[:, lanes] * signal.astype(F32)
                gated = gated * silu_gate_ref[flip, :, lanes]
                squares = squares + gated * gated
                gated_ref[chain, :, lanes] = gated
            scale = lax.rsqrt(jnp.sum(squares, axis=1, keepdims=True) * (1.0 / E) + eps)
            for pair in range(PAIRS):
                lanes = lanes_of(pair)
                gated_ref[chain, :, lanes] = (
                    gated_ref[chain, :, lanes] * scale * gate_gain_ref[:, lanes]
                )

    normed = gated_ref[...].astype(BF16).reshape(4 * BLOCK, E)
    made = dot(normed, output_weight_ref[...])
    straight, crossed = made[: 2 * BLOCK], made[2 * BLOCK :]
    high, low = split(crossed, 2)
    both = straight + flip_lanes(high, swap) + flip_lanes(low, swap)
    backward = both[BLOCK:].astype(BF16).astype(F32)
    out_ref[...] = (both[:BLOCK] + backward).astype(BF16)


def wide_row(row):
    select = (iota((HEADS, E), 1) // N == iota((HEADS, E), 0)).astype(BF16)
    return exact_dot(jnp.broadcast_to(row, (8, HEADS)), select)[:1]


def swapped(rows, step, count):
    return lax.ppermute(rows, "seq", [(i, i ^ step) for i in range(count)])


def on_device(
    hidden,
    norm_gain,
    input_weight,
    step_weight,
    conv_weight,
    conv_bias,
    step_bias,
    log_rate,
    skip_gain,
    gate_gain,
    output_weight,
):
    count = lax.axis_size("seq")
    top = count // 2
    row = lambda vector: vector.reshape(1, -1)
    whole = pl.BlockSpec(memory_space=pltpu.VMEM)
    shape = jax.ShapeDtypeStruct
    gain, step_map = row(norm_gain), step_weight.T
    step_bias, log_rate = row(step_bias), row(log_rate)
    across = swapped(hidden, top, count)

    def call(kernel, name, outs, scratch, operands, flops, limit, spec=whole):
        return pl.pallas_call(
            kernel,
            out_shape=outs,
            in_specs=[spec] * len(operands),
            out_specs=[whole] * len(outs),
            scratch_shapes=scratch,
            compiler_params=pltpu.CompilerParams(vmem_limit_bytes=limit * 2**20),
            cost_estimate=pl.CostEstimate(
                flops=flops, bytes_accessed=10**7, transcendentals=10**6
            ),
            name=name,
        )(*operands)

    small = (hidden, gain, step_map, step_bias, log_rate)
    normal, decay, lift = call(
        decay_kernel,
        "decays",
        [
            shape((2 * BLOCK, EMBED), BF16),
            shape((2, HEADS, BLOCK, BLOCK), F32),
            shape((4, BLOCK, E), F32),
        ],
        [
            *[pltpu.VMEM(part.shape, part.dtype) for part in small],
            pltpu.SemaphoreType.DMA((5,)),
        ],
        [pltpu.with_memory_space_constraint(part, pltpu.HBM) for part in small],
        10**9,
        12,
        pl.BlockSpec(memory_space=pltpu.HBM),
    )
    own = call(
        own_kernel,
        "own_rows",
        [
            shape((4, BLOCK, MIXED), BF16),
            shape((2, 2 * EDGE, MIXED), F32),
            shape((2, BLOCK, E), F32),
        ],
        [pltpu.VMEM((2, TILES, BLOCK + 2 * PAD, 128), F32)],
        [normal, input_weight, conv_weight, conv_bias],
        10**9,
        12,
    )
    start, across, decay, lift, *own = lax.optimization_barrier(
        (hidden, across, decay, lift, *own)
    )
    received = {0: start, top: across}
    for bit in reversed(range(top.bit_length() - 1)):
        for mask in sorted(received):
            received[mask | 1 << bit] = swapped(received[mask], 1 << bit, count)
    shared = [gain, input_weight, step_map, conv_weight, conv_bias, step_bias, log_rate]
    ahead = call(
        functools.partial(ahead_kernel, top),
        "across_rows",
        [
            shape((2, BLOCK, MIXED), BF16),
            shape((2, EDGE + PAD, MIXED), F32),
            shape((HEADS, 2 * BLOCK), F32),
        ],
        [pltpu.VMEM((2, TILES, PAD + BLOCK, 128), F32)],
        [across, *shared],
        10**9,
        12,
    )
    others = [mask for mask in range(1, count) if mask != top]
    (out,) = call(
        functools.partial(join_kernel, count, top),
        "join_blocks",
        [shape((BLOCK, EMBED), BF16)],
        [
            pltpu.VMEM((2 * len(others) * BLOCK, EMBED), BF16),
            pltpu.VMEM((2 * len(others), TILES, PAD + BLOCK, 128), F32),
            pltpu.VMEM((count - 1, 2, PAD, MIXED), F32),
            pltpu.VMEM((4, 2 * N, E), BF16),
            pltpu.VMEM((4, PAD + EDGE, MIXED), F32),
            pltpu.VMEM((2, TILES, PAD + EDGE, 128), F32),
            pltpu.VMEM((4, BLOCK, E), F32),
        ],
        [
            *[received[mask] for mask in others],
            *shared,
            row(skip_gain),
            row(gate_gain),
            output_weight,
            decay,
            lift,
            *own,
            *ahead,
        ],
        2 * 10**9,
        18 + 2 * len(others),
    )
    return out


def solution(mesh):
    in_specs = (P(("batch", "seq"), None), P(), P(), P(), P(), P(), P(), P(), P(), P(), P())
    out_specs = P(("batch", "seq"), None)
    return jax.shard_map(
        on_device, mesh=mesh, in_specs=in_specs, out_specs=out_specs, check_vma=False
    )
```

time: 24 us -> 16.6 us (0.69); the launches traced: 23.6 us -> 16.5 us
  local copies, waits for them, and re-layouts: 6.81 us -> 0.06 us
  starting transfers between devices: 4.76 us -> 3.57 us
  Pallas kernels: 11.9 us -> 12.7 us
    unnamed x27 -> x22, local copies, waits for them, and re-layouts: 6.11 us -> 0.06 us
    ppermute x3, starting transfers between devices: 4.76 us -> 3.57 us  [swapped(): return lax.ppermute(rows, 'seq', [(i, i ^ step) for i in range(count)])]
    pallas_call x2 -> x4, Pallas kernels: 11.9 us -> 12.7 us  [call(): pl.pallas_call(kernel, out_shape=outs, in_specs=[spec] * len(operands), o...]
    reshape x1 -> x0, local copies, waits for them, and re-layouts: 0.7 us -> none  [on_device(): row = lambda vector: vector.reshape(1, -1)]
  transfers between devices with their start and end apart: 3 -> 3, of which waited for: 0 -> 0; matrix products, arithmetic and copies ran while one was open for 7% -> 0% of each run, Pallas kernels for 15% -> 34%
where the time goes in v1:
time: 16.6 us; the launch traced here: 16.5 us
  Pallas kernels  12.7 us (77%)
  starting transfers between devices  3.57 us (22%)
  between operations  0.18 us (1%)
    pallas_call x4, Pallas kernels, call(): pl.pallas_call(kernel, out_shape=outs, in_specs=[spec] * len(operands), o...  12.7 us
    ppermute x3, starting transfers between devices, swapped(): return lax.ppermute(rows, 'seq', [(i, i ^ step) for i in range(count)])  3.57 us
  transfers between devices with their start and end apart: 3, of which 0 were waited for; matrix products, arithmetic and copies ran while one was open for 0% of the time, Pallas kernels for 34%

profile of v1, /device:TPU:0, one launch (start us, length us, event | category | flops | bytes accessed | tf_op | source)
XLA Modules:
  0.0 16.5 jit_solution(4920630009290887162)
XLA Ops:
  0.0 0.0 copy-start.4
  0.0 0.0 copy-start.2
  0.0 0.0 copy-start
  0.0 3.0 %collective-permute-start = (bf16[128,512]{1,0:T(8,128)(2,1)}, bf16[128,512]{1,0:T(8,128)(2,1)S(1)}, u32[]{:S(2)}, u32[]{:S(2)}) collective-permute-start(bf16[128,512]{1,0:T(8,128)(2,1)} %refs_0_.1), channel_id=1, source_target_pairs={{0,16},{8,24},{16,0},{24,8},{1,17},{9,25},{17,1},{25,9},{2,18},{10... | collective-permute-start | bytes 393224 | tf_op jit(solution)/shard_map/ppermute | solution.py:450
  3.0 2.7 %decays.1 = (bf16[256,512]{1,0:T(8,128)(2,1)S(1)}, f32[2,16,128,128]{3,2,1,0:T(8,128)S(1)}, f32[4,128,1024]{2,1,0:T(8,128)S(1)}) custom-call(bf16[128,512]{1,0:T(8,128)(2,1)} %refs_0_.1, f32[1,512]{1,0:T(1,128)} %bitcast.10, bf16[16,512]{1,0:T(8,128)(2,1)} %bitcast.6, f32[1,16]{1,0:T(1,128)} %bitcast.13, f32[1,16]{1,0:T(1,128)} %bitcast.16), custom_call_target="tpu_custom_call" | custom-call | flops 1000000000 | bytes 10000000 | tf_op jit(solution)/shard_map/decays/pallas_call | solution.py:476
  5.7 0.0 copy-start.10
  5.7 0.0 copy-start.3
  5.7 0.0 copy-start.6
  5.7 0.0 copy-start.7
  5.7 0.0 copy-start.8
  5.7 0.0 copy-done.4
  5.8 0.0 copy-done.2
  5.8 0.0 copy-done
  5.8 1.7 %own_rows.1 = (bf16[4,128,1152]{2,1,0:T(8,128)(2,1)S(1)}, f32[2,32,1152]{2,1,0:T(8,128)S(1)}, f32[2,128,1024]{2,1,0:T(8,128)S(1)}) custom-call(bf16[256,512]{1,0:T(8,128)(2,1)S(1)} %get-tuple-element.23.normal_ref, bf16[512,2176]{1,0:T(8,128)(2,1)S(1)} %copy-done, f32[4,1152]{1,0:T(4,128)S(1)} %copy-done.2, f32[1152]{0:T(1024)S(1)} %copy-done.4), custom_call_target="tpu_custom_call" | custom-call | flops 1000000000 | bytes 10000000 | tf_op jit(solution)/shard_map/own_rows/pallas_call | solution.py:476
  7.5 0.0 copy-start.1
  7.5 0.0 copy-start.5
  7.5 0.0 copy-start.9
  7.5 0.0 collective-permute-done.block_ref
  7.5 0.0 copy-done.10
  7.5 0.1 collective-permute-start.1
  7.6 0.5 %collective-permute-start.2 = (bf16[128,512]{1,0:T(8,128)(2,1)S(1)}, bf16[128,512]{1,0:T(8,128)(2,1)S(1)}, u32[]{:S(2)}, u32[]{:S(2)}) collective-permute-start(bf16[128,512]{1,0:T(8,128)(2,1)S(1)} %collective-permute-done.block_ref), channel_id=1, source_target_pairs={{0,8},{8,0},{16,24},{24,16},{1,9},{9,1},{17,25},{25,17},{2,10},{10... | collective-permute-start | bytes 393224 | tf_op jit(solution)/shard_map/ppermute | solution.py:450
  8.1 0.0 copy-done.3
  8.1 0.0 copy-done.6
  8.1 0.0 copy-done.7
  8.1 0.0 copy-done.8
  8.1 1.2 %across_rows.1 = (bf16[2,128,1152]{2,1,0:T(8,128)(2,1)S(1)}, f32[2,24,1152]{2,1,0:T(8,128)S(1)}, f32[16,256]{1,0:T(8,128)S(1)}) custom-call(bf16[128,512]{1,0:T(8,128)(2,1)S(1)} %collective-permute-done.block_ref, f32[1,512]{1,0:T(1,128)S(1)} %bitcast.11, bf16[512,2176]{1,0:T(8,128)(2,1)S(1)} %copy-done, bf16[16,512]{1,0:T(8,128)(2,1)S(1)} %bitcast.7, ...), custom_call_target="tpu_custom_call" | custom-call | flops 1000000000 | bytes 10000000 | tf_op jit(solution)/shard_map/across_rows/pallas_call | solution.py:476
  9.3 0.0 collective-permute-done.1.refs_0_
  9.3 0.0 collective-permute-done.2.refs_1_
  9.3 0.0 copy-done.1
  9.4 0.0 copy-done.5
  9.4 0.0 copy-done.9
  9.4 7.1 %join_blocks.1 = bf16[128,512]{1,0:T(8,128)(2,1)} custom-call(bf16[128,512]{1,0:T(8,128)(2,1)S(1)} %collective-permute-done.1.refs_0_, bf16[128,512]{1,0:T(8,128)(2,1)S(1)} %collective-permute-done.2.refs_1_, f32[1,512]{1,0:T(1,128)S(1)} %bitcast.12, bf16[512,2176]{1,0:T(8,128)(2,1)S(1)} %copy-done, bf16[16,512]{1,0:T(8,128)(2,1)S(1)} %bitcast.8, ...), custom_call_target="tpu_custom_call" | custom-call | flops 2000000000 | bytes 10000000 | tf_op jit(solution)/shard_map/join_blocks/pallas_call | solution.py:476
Async XLA Ops:
  0.0 5.7 %copy-start.4 = (f32[1152]{0:T(1024)S(1)}, f32[1152]{0:T(1024)}, u32[]{:S(2)}) copy-start(f32[1152]{0:T(1024)} %refs_6_.1) | copy-start | bytes 13828
  0.0 5.8 %copy-start.2 = (f32[4,1152]{1,0:T(4,128)S(1)}, f32[4,1152]{1,0:T(4,128)}, u32[]{:S(2)}) copy-start(f32[4,1152]{1,0:T(4,128)} %refs_5_.1) | copy-start | bytes 55300
  0.0 5.8 %copy-start = (bf16[512,2176]{1,0:T(8,128)(2,1)S(1)}, bf16[512,2176]{1,0:T(8,128)(2,1)}, u32[]{:S(2)}) copy-start(bf16[512,2176]{1,0:T(8,128)(2,1)} %refs_3_.1) | copy-start | bytes 6684676
  0.0 7.5 %collective-permute-start = (bf16[128,512]{1,0:T(8,128)(2,1)}, bf16[128,512]{1,0:T(8,128)(2,1)S(1)}, u32[]{:S(2)}, u32[]{:S(2)}) collective-permute-start(bf16[128,512]{1,0:T(8,128)(2,1)} %refs_0_.1), channel_id=1, source_target_pairs={{0,16},{8,24},{16,0},{24,8},{1,17},{9,25},{17,1},{25,9},{2,18},{10... | collective-permute-start | bytes 393224 | tf_op jit(solution)/shard_map/ppermute | solution.py:450
  5.7 1.9 %copy-start.10 = (bf16[128,512]{1,0:T(8,128)(2,1)S(1)}, bf16[128,512]{1,0:T(8,128)(2,1)}, u32[]{:S(2)}) copy-start(bf16[128,512]{1,0:T(8,128)(2,1)} %refs_0_.1) | copy-start | bytes 393220
  5.7 2.4 %copy-start.3 = (bf16[512,16]{0,1:T(8,128)(2,1)S(1)}, bf16[512,16]{0,1:T(8,128)(2,1)}, u32[]{:S(2)}) copy-start(bf16[512,16]{0,1:T(8,128)(2,1)} %param.14) | copy-start | bytes 49156
  5.7 2.4 %copy-start.6 = (f32[512]{0:T(512)S(1)}, f32[512]{0:T(512)}, u32[]{:S(2)}) copy-start(f32[512]{0:T(512)} %param.12) | copy-start | bytes 6148
  5.7 2.4 %copy-start.7 = (f32[16]{0:T(128)S(1)}, f32[16]{0:T(128)}, u32[]{:S(2)}) copy-start(f32[16]{0:T(128)} %param.17) | copy-start | bytes 196
  5.7 2.4 %copy-start.8 = (f32[16]{0:T(128)S(1)}, f32[16]{0:T(128)}, u32[]{:S(2)}) copy-start(f32[16]{0:T(128)} %param.18) | copy-start | bytes 196
  7.5 1.9 %copy-start.1 = (bf16[1024,512]{1,0:T(8,128)(2,1)S(1)}, bf16[1024,512]{1,0:T(8,128)(2,1)}, u32[]{:S(2)}) copy-start(bf16[1024,512]{1,0:T(8,128)(2,1)} %refs_11_.1) | copy-start | bytes 3145732
  7.5 1.9 %copy-start.5 = (f32[1024]{0:T(1024)S(1)}, f32[1024]{0:T(1024)}, u32[]{:S(2)}) copy-start(f32[1024]{0:T(1024)} %param.20) | copy-start | bytes 12292
  7.5 1.9 %copy-start.9 = (f32[16]{0:T(128)S(1)}, f32[16]{0:T(128)}, u32[]{:S(2)}) copy-start(f32[16]{0:T(128)} %param.19) | copy-start | bytes 196
  7.5 1.8 %collective-permute-start.1 = (bf16[128,512]{1,0:T(8,128)(2,1)S(1)}, bf16[128,512]{1,0:T(8,128)(2,1)S(1)}, u32[]{:S(2)}, u32[]{:S(2)}) collective-permute-start(bf16[128,512]{1,0:T(8,128)(2,1)S(1)} %copy-done.10), channel_id=1, source_target_pairs={{0,8},{8,0},{16,24},{24,16},{1,9},{9,1},{17,25},{25,17},{2,10},{10... | collective-permute-start | bytes 393224 | tf_op jit(solution)/shard_map/ppermute | solution.py:450
  7.6 1.7 %collective-permute-start.2 = (bf16[128,512]{1,0:T(8,128)(2,1)S(1)}, bf16[128,512]{1,0:T(8,128)(2,1)S(1)}, u32[]{:S(2)}, u32[]{:S(2)}) collective-permute-start(bf16[128,512]{1,0:T(8,128)(2,1)S(1)} %collective-permute-done.block_ref), channel_id=1, source_target_pairs={{0,8},{8,0},{16,24},{24,16},{1,9},{9,1},{17,25},{25,17},{2,10},{10... | collective-permute-start | bytes 393224 | tf_op jit(solution)/shard_map/ppermute | solution.py:450

commit v2 on v1

--- a/solution.py
+++ b/solution.py
@@ -88,12 +88,19 @@
     return -jnp.exp(column_of(log_rate)) * (jnp.maximum(v, 0.0) + rest)
 
 
-def spread_heads(values, terms, start, stop, each):
-    parts = jnp.concatenate(split(values, terms), axis=0)
-    shape = (terms * HEADS, stop - start)
-    head = (iota(shape, 1) + start) // each
-    select = (iota(shape, 0) % HEADS == head).astype(BF16)
-    return lax.dot_general(parts, select, (((0,), (0,)), ((), ())), preferred_element_type=F32)
+def selectors(terms, heads):
+    shape = (terms * HEADS, 256)
+    head = iota(shape, 0) & (HEADS - 1)
+    near = iota(shape, 1) >> (8 - (heads.bit_length() - 1))
+    return [(head - near == low).astype(BF16) for low in range(0, HEADS, heads)]
+
+
+def stacked_split(values, terms):
+    return jnp.concatenate(split(values, terms), axis=0)
+
+
+def dot_columns(a, b):
+    return lax.dot_general(a, b, (((0,), (0,)), ((), ())), preferred_element_type=F32)
 
 
 def lanes_of(tile):
@@ -135,26 +142,31 @@
     both = jnp.concatenate([log_decay[:, :BLOCK], log_decay[:, BLOCK:]], axis=0)
     before = exact_dot(both, (row <= column).astype(BF16))
     after = exact_dot(both, (row >= column).astype(BF16))
+    twos, fours = selectors(3, 2), selectors(1, 4)
     for flip in range(2):
         heads = slice(flip * HEADS, (flip + 1) * HEADS)
+        ones = jnp.ones((3 * HEADS, BLOCK), BF16)
+        sides = []
+        for rows in (before, after):
+            parts = stacked_split(rows[heads], 3)
+            sides.append((jnp.concatenate([parts, ones], axis=0), jnp.concatenate([-parts] * 2, 1)))
+
+        def spread(side, pair):
+            plus, minus = sides[side]
+            return dot_columns(plus, jnp.concatenate([twos[pair], twos[pair] * minus], axis=0))
+
         for pair in range(PAIRS):
-            low, high = 2 * pair * BLOCK, 2 * (pair + 1) * BLOCK
-            from_start = spread_heads(before[heads], 3, low, high, BLOCK)
-            to_end = spread_heads(after[heads], 3, low, high, BLOCK)
+            from_start, to_end = spread(0, pair), spread(1, pair)
             for near in range(2):
-                at = flip * HEADS + 2 * pair + near
                 lanes = lanes_of(near)
                 decay_ref[flip, 2 * pair + near] = jnp.exp(
-                    jnp.where(
-                        lower,
-                        from_start[:, lanes] - before[at : at + 1],
-                        to_end[:, lanes] - after[at : at + 1],
-                    )
-                )
-        for start, stop in chunks(E):
-            for way, rows in enumerate((before, after)):
-                lift_ref[2 * flip + way, :, start:stop] = spread_heads(
-                    jnp.exp(rows[heads]), 2, start, stop, N
+                    jnp.where(lower, from_start[:, lanes], to_end[:, lanes])
+                ).astype(BF16)
+        for way, rows in enumerate((before, after)):
+            lifts = jnp.exp(rows[heads]).astype(BF16)
+            for place, (start, stop) in enumerate(chunks(E)):
+                lift_ref[2 * flip + way, :, start:stop] = dot_columns(lifts, fours[place]).astype(
+                    BF16
                 )
 
 
@@ -171,7 +183,7 @@
     normal = normal_ref[...]
     taps, bias = 0.5 * conv_weight_ref[...], 0.5 * conv_bias_ref[...].reshape(1, MIXED)
     for start, stop in chunks(MIXED):
-        mixed = dot(normal, input_weight_ref[:, E + start : E + stop]).astype(BF16).astype(F32)
+        mixed = dot(normal, input_weight_ref[:, E + start : E + stop])
         for flip in range(2):
             rows = mixed[flip * BLOCK : (flip + 1) * BLOCK]
             edge_ref[flip, :EDGE, start:stop] = rows[:EDGE]
@@ -186,7 +198,7 @@
                     half = filtered(place, PAD, lanes, taps, bias, way == 1)
                     activated_ref[2 * flip + way, :, lanes] = half_silu(half).astype(BF16)
     for start, stop in chunks(E):
-        gate = dot(normal, input_weight_ref[:, start:stop]).astype(BF16).astype(F32)
+        gate = dot(normal, input_weight_ref[:, start:stop])
         gate = half_silu(0.5 * gate)
         for flip in range(2):
             silu_gate_ref[flip, :, start:stop] = gate[flip * BLOCK : (flip + 1) * BLOCK]
@@ -222,7 +234,7 @@
     )
     taps, bias = 0.5 * conv_weight_ref[...], 0.5 * conv_bias_ref[...].reshape(1, MIXED)
     for start, stop in chunks(MIXED):
-        mixed = dot(normal, input_weight_ref[:, E + start : E + stop]).astype(BF16).astype(F32)
+        mixed = dot(normal, input_weight_ref[:, E + start : E + stop])
         for flip in range(2):
             rows = mixed[flip * BLOCK : (flip + 1) * BLOCK]
             edge_ref[flip, :EDGE, start:stop] = rows[:EDGE]
@@ -261,7 +273,6 @@
         out_ref,
         normal_ref,
         extended_ref,
-        halo_ref,
         memory_ref,
         window_ref,
         patch_ref,
@@ -271,13 +282,14 @@
     swap = reversal()
     row, column = iota((BLOCK, BLOCK), 0), iota((BLOCK, BLOCK), 1)
     lower, upper = row >= column, row <= column
-    left = column < N
+    left, right = (column < N).astype(BF16), (column >= N).astype(BF16)
     taps, bias = 0.5 * conv_weight_ref[...], 0.5 * conv_bias_ref[...].reshape(1, MIXED)
 
-    def halo_of(block, flip):
-        exists = jnp.where((block >= 0) & (block < count), 1.0, 0.0)
-        place = jnp.clip((block ^ index) - 1, 0, count - 2)
-        return exists * halo_ref[place, flip]
+    def picked(rows, block):
+        result = jnp.zeros((PAD, rows[top].shape[1]), F32)
+        for mask, part in rows.items():
+            result = jnp.where((index ^ mask) == block, part, result)
+        return result
 
     for place, mask in enumerate(others):
         block = received[place][...]
@@ -311,24 +323,41 @@
                 )
                 tail = tail + jnp.where(later, wholes[other, flip], 0.0)
         faded[flip].append(jnp.exp(tail))
-    faded = [jnp.concatenate(rows, axis=1) for rows in faded]
-
-    for flip in range(2):
-        halo_ref[top - 1, flip] = ahead_edge_ref[flip, EDGE:]
+    faded = [jnp.concatenate(rows, axis=1).astype(BF16) for rows in faded]
+    fours = selectors(1, 4)
+
     writers = [None, None]
     order = chunks(MIXED)
-    for start, stop in order[-1:] + order[:-1]:
-        mixed = dot(normal, input_weight_ref[:, E + start : E + stop]).astype(BF16).astype(F32)
-        for place, mask in enumerate(others):
-            for flip in range(2):
+    order = order[-1:] + order[:-1]
+
+    def project(place):
+        start, stop = order[place]
+        return dot(normal, input_weight_ref[:, E + start : E + stop])
+
+    def fade_of(place, flip):
+        return dot_columns(faded[flip], fours[order[place][0] // 256]).astype(BF16)
+
+    ready, coming = project(0), None
+    for turn, (start, stop) in enumerate(order):
+        mixed = ready
+        if turn + 1 < len(order):
+            ready = project(turn + 1)
+            fades, coming = coming, [fade_of(turn + 1, flip) for flip in range(2)]
+        else:
+            fades = coming
+        for flip in range(2):
+            acted, last = {}, {top: ahead_edge_ref[flip, EDGE:, start:stop]}
+            for place, mask in enumerate(others):
                 low = (2 * place + flip) * BLOCK
-                halo_ref[mask - 1, flip, :, start:stop] = mixed[low + BLOCK - PAD : low + BLOCK]
-        for flip in range(2):
-            acted = {}
+                last[mask] = mixed[low + BLOCK - PAD : low + BLOCK]
+            window_ref[2 * flip, :PAD, start:stop] = picked(last, index - 1)
+            behind = picked(last, index + 1)
+            for step in range(K - 1):
+                spot = slice(EDGE + step, EDGE + step + 1)
+                window_ref[2 * flip + 1, spot, start:stop] = behind[PAD - 1 - step : PAD - step]
             for mask in range(1, count):
                 block = index ^ mask
-                before = jnp.where(block < index, block - 1, block + 1)
-                halo = halo_of(before, flip)[:, start:stop]
+                halo = picked(last, jnp.where(block < index, block - 1, block + 1))
                 if mask == top:
                     near = []
                     for tile in range(start // 128, stop // 128):
@@ -363,16 +392,18 @@
                     sides.append(jnp.concatenate([maps * earlier, maps * later], axis=0))
                 writers[flip] = jnp.concatenate(sides, axis=1)
                 continue
-            fade = spread_heads(faded[flip], 2, start, stop, N)
+            fade = fades[flip]
             decayed = [
-                (fade[at * BLOCK : (at + 1) * BLOCK] * acted[at + 1].astype(F32)).astype(BF16)
+                fade[at * BLOCK : (at + 1) * BLOCK] * acted[at + 1]
                 for at in range(count - 1)
             ]
             memory = dot(writers[flip], jnp.concatenate(decayed, axis=0))
             for way in range(2):
-                high, low = split(memory[way * N : (way + 1) * N], 2)
-                memory_ref[2 * flip + way, :N, start:stop] = high
-                memory_ref[2 * flip + way, N:, start:stop] = low
+                kept = memory[way * N : (way + 1) * N]
+                even = (iota(kept.shape, 1) & N) == 0
+                chain = 2 * flip + way
+                memory_ref[chain, :N, start:stop] = jnp.where(even, kept, 0.0).astype(BF16)
+                memory_ref[chain, N:, start:stop] = jnp.where(even, 0.0, kept).astype(BF16)
 
     skip = wide_row(skip_gain_ref[...])
     for flip in range(2):
@@ -380,13 +411,9 @@
             chain = 2 * flip + way
             spot = window_ref.at[chain]
             if way == 0:
-                spot[:PAD] = halo_of(index - 1, flip)
                 spot[PAD:] = edge_ref[flip, :EDGE]
             else:
-                halo = halo_of(index + 1, flip)
                 spot[:EDGE] = edge_ref[flip, EDGE:]
-                for step in range(K - 1):
-                    spot[EDGE + step : EDGE + step + 1] = halo[PAD - 1 - step : PAD - step]
             at = PAD if way == 0 else 0
             half = filtered(spot, at, slice(0, MIXED), taps, bias, way == 1, EDGE)
             patch = half_silu(half).astype(BF16)
@@ -402,25 +429,24 @@
             maps = acted(PAIRS)
             writer, reader = maps[:, :N], maps[:, N:]
             scores = jnp.where(lower if way == 0 else upper, dot_rows(reader, writer), 0.0)
+            scores = scores.astype(BF16)
             squares = jnp.zeros((BLOCK, 128), F32)
             doubled = jnp.concatenate([reader, reader], axis=1)
             for pair in range(PAIRS):
                 lanes = lanes_of(pair)
                 signal = acted(pair)
-                zeros = jnp.zeros_like(signal)
                 signals = jnp.concatenate(
-                    [jnp.where(left, signal, zeros), jnp.where(left, zeros, signal)], axis=0
+                    [signal * left, signal * right, memory_ref[chain, :, lanes]], axis=0
                 )
                 weights = jnp.concatenate(
                     [
-                        (decay_ref[flip, 2 * pair + near] * scores).astype(BF16)
+                        decay_ref[flip, 2 * pair + near] * scores
                         for near in range(2)
-                    ],
+                    ]
+                    + [lift_ref[chain, :, lanes] * doubled],
                     axis=1,
                 )
                 inside = dot(weights, signals)
-                carried = dot(doubled, memory_ref[chain, :, lanes])
-                inside = inside + lift_ref[chain, :, lanes] * carried
                 gated = inside + skip[:, lanes] * signal.astype(F32)
                 gated = gated * silu_gate_ref[flip, :, lanes]
                 squares = squares + gated * gated
@@ -492,8 +518,8 @@
         "decays",
         [
             shape((2 * BLOCK, EMBED), BF16),
-            shape((2, HEADS, BLOCK, BLOCK), F32),
-            shape((4, BLOCK, E), F32),
+            shape((2, HEADS, BLOCK, BLOCK), BF16),
+            shape((4, BLOCK, E), BF16),
         ],
         [
             *[pltpu.VMEM(part.shape, part.dtype) for part in small],
@@ -546,7 +572,6 @@
         [
             pltpu.VMEM((2 * len(others) * BLOCK, EMBED), BF16),
             pltpu.VMEM((2 * len(others), TILES, PAD + BLOCK, 128), F32),
-            pltpu.VMEM((count - 1, 2, PAD, MIXED), F32),
             pltpu.VMEM((4, 2 * N, E), BF16),
             pltpu.VMEM((4, PAD + EDGE, MIXED), F32),
             pltpu.VMEM((2, TILES, PAD + EDGE, 128), F32),

time: 16.6 us -> 15.2 us (0.916)
  Pallas kernels: 12.7 us -> 11.2 us
    pallas_call x4, Pallas kernels: 12.7 us -> 11.2 us  [call(): pl.pallas_call(kernel, out_shape=outs, in_specs=[spec] * len(operands), o...]
  transfers between devices with their start and end apart: 3 -> 3, of which waited for: 0 -> 0; matrix products, arithmetic and copies ran while one was open for 0% -> 0% of each run, Pallas kernels for 34% -> 35%
where the time goes in v2:
time: 15.2 us; the launch traced here: 15.1 us
  Pallas kernels  11.2 us (74%)
  starting transfers between devices  3.57 us (23%)
  between operations  0.18 us (1%)
    pallas_call x4, Pallas kernels, call(): pl.pallas_call(kernel, out_shape=outs, in_specs=[spec] * len(operands), o...  11.2 us
    ppermute x3, starting transfers between devices, swapped(): return lax.ppermute(rows, 'seq', [(i, i ^ step) for i in range(count)])  3.57 us
  transfers between devices with their start and end apart: 3, of which 0 were waited for; matrix products, arithmetic and copies ran while one was open for 0% of the time, Pallas kernels for 35%

profile of v2, /device:TPU:0, one launch (start us, length us, event | category | flops | bytes accessed | tf_op | source)
XLA Modules:
  0.0 15.1 jit_solution(9646117504203409818)
XLA Ops:
  0.0 0.0 copy-start.4
  0.0 0.0 copy-start.2
  0.0 0.0 copy-start
  0.0 3.0 %collective-permute-start = (bf16[128,512]{1,0:T(8,128)(2,1)}, bf16[128,512]{1,0:T(8,128)(2,1)S(1)}, u32[]{:S(2)}, u32[]{:S(2)}) collective-permute-start(bf16[128,512]{1,0:T(8,128)(2,1)} %refs_0_.1), channel_id=1, source_target_pairs={{0,16},{8,24},{16,0},{24,8},{1,17},{9,25},{17,1},{25,9},{2,18},{10... | collective-permute-start | bytes 393224 | tf_op jit(solution)/shard_map/ppermute | solution.py:476
  3.0 2.6 %decays.1 = (bf16[256,512]{1,0:T(8,128)(2,1)S(1)}, bf16[2,16,128,128]{3,2,1,0:T(8,128)(2,1)S(1)}, bf16[4,128,1024]{2,1,0:T(8,128)(2,1)S(1)}) custom-call(bf16[128,512]{1,0:T(8,128)(2,1)} %refs_0_.1, f32[1,512]{1,0:T(1,128)} %bitcast.10, bf16[16,512]{1,0:T(8,128)(2,1)} %bitcast.6, f32[1,16]{1,0:T(1,128)} %bitcast.13, f32[1,16]{1,0:T(1,128)} %bitcast.16), custom_call_target="tpu_custom_call" | custom-call | flops 1000000000 | bytes 10000000 | tf_op jit(solution)/shard_map/decays/pallas_call | solution.py:502
  5.6 0.0 copy-start.10
  5.6 0.0 copy-start.3
  5.7 0.0 copy-start.6
  5.7 0.0 copy-start.7
  5.7 0.0 copy-start.8
  5.7 0.0 copy-done.4
  5.7 0.0 copy-done.2
  5.7 0.0 copy-done
  5.7 1.6 %own_rows.1 = (bf16[4,128,1152]{2,1,0:T(8,128)(2,1)S(1)}, f32[2,32,1152]{2,1,0:T(8,128)S(1)}, f32[2,128,1024]{2,1,0:T(8,128)S(1)}) custom-call(bf16[256,512]{1,0:T(8,128)(2,1)S(1)} %get-tuple-element.23.normal_ref, bf16[512,2176]{1,0:T(8,128)(2,1)S(1)} %copy-done, f32[4,1152]{1,0:T(4,128)S(1)} %copy-done.2, f32[1152]{0:T(1024)S(1)} %copy-done.4), custom_call_target="tpu_custom_call" | custom-call | flops 1000000000 | bytes 10000000 | tf_op jit(solution)/shard_map/own_rows/pallas_call | solution.py:502
  7.3 0.0 copy-start.1
  7.3 0.0 copy-start.5
  7.4 0.0 copy-start.9
  7.4 0.0 collective-permute-done.block_ref
  7.4 0.0 copy-done.10
  7.4 0.1 collective-permute-start.1
  7.5 0.5 %collective-permute-start.2 = (bf16[128,512]{1,0:T(8,128)(2,1)S(1)}, bf16[128,512]{1,0:T(8,128)(2,1)S(1)}, u32[]{:S(2)}, u32[]{:S(2)}) collective-permute-start(bf16[128,512]{1,0:T(8,128)(2,1)S(1)} %collective-permute-done.block_ref), channel_id=1, source_target_pairs={{0,8},{8,0},{16,24},{24,16},{1,9},{9,1},{17,25},{25,17},{2,10},{10... | collective-permute-start | bytes 393224 | tf_op jit(solution)/shard_map/ppermute | solution.py:476
  8.0 0.0 copy-done.3
  8.0 0.0 copy-done.6
  8.0 0.0 copy-done.7
  8.0 0.0 copy-done.8
  8.0 1.0 %across_rows.1 = (bf16[2,128,1152]{2,1,0:T(8,128)(2,1)S(1)}, f32[2,24,1152]{2,1,0:T(8,128)S(1)}, f32[16,256]{1,0:T(8,128)S(1)}) custom-call(bf16[128,512]{1,0:T(8,128)(2,1)S(1)} %collective-permute-done.block_ref, f32[1,512]{1,0:T(1,128)S(1)} %bitcast.11, bf16[512,2176]{1,0:T(8,128)(2,1)S(1)} %copy-done, bf16[16,512]{1,0:T(8,128)(2,1)S(1)} %bitcast.7, ...), custom_call_target="tpu_custom_call" | custom-call | flops 1000000000 | bytes 10000000 | tf_op jit(solution)/shard_map/across_rows/pallas_call | solution.py:502
  9.0 0.0 collective-permute-done.1.refs_0_
  9.0 0.0 collective-permute-done.2.refs_1_
  9.0 0.0 copy-done.1
  9.0 0.0 copy-done.5
  9.1 0.0 copy-done.9
  9.1 6.0 %join_blocks.1 = bf16[128,512]{1,0:T(8,128)(2,1)} custom-call(bf16[128,512]{1,0:T(8,128)(2,1)S(1)} %collective-permute-done.1.refs_0_, bf16[128,512]{1,0:T(8,128)(2,1)S(1)} %collective-permute-done.2.refs_1_, f32[1,512]{1,0:T(1,128)S(1)} %bitcast.12, bf16[512,2176]{1,0:T(8,128)(2,1)S(1)} %copy-done, bf16[16,512]{1,0:T(8,128)(2,1)S(1)} %bitcast.8, ...), custom_call_target="tpu_custom_call" | custom-call | flops 2000000000 | bytes 10000000 | tf_op jit(solution)/shard_map/join_blocks/pallas_call | solution.py:502
Async XLA Ops:
  0.0 5.7 %copy-start.4 = (f32[1152]{0:T(1024)S(1)}, f32[1152]{0:T(1024)}, u32[]{:S(2)}) copy-start(f32[1152]{0:T(1024)} %refs_6_.1) | copy-start | bytes 13828
  0.0 5.7 %copy-start.2 = (f32[4,1152]{1,0:T(4,128)S(1)}, f32[4,1152]{1,0:T(4,128)}, u32[]{:S(2)}) copy-start(f32[4,1152]{1,0:T(4,128)} %refs_5_.1) | copy-start | bytes 55300
  0.0 5.7 %copy-start = (bf16[512,2176]{1,0:T(8,128)(2,1)S(1)}, bf16[512,2176]{1,0:T(8,128)(2,1)}, u32[]{:S(2)}) copy-start(bf16[512,2176]{1,0:T(8,128)(2,1)} %refs_3_.1) | copy-start | bytes 6684676
  0.0 7.4 %collective-permute-start = (bf16[128,512]{1,0:T(8,128)(2,1)}, bf16[128,512]{1,0:T(8,128)(2,1)S(1)}, u32[]{:S(2)}, u32[]{:S(2)}) collective-permute-start(bf16[128,512]{1,0:T(8,128)(2,1)} %refs_0_.1), channel_id=1, source_target_pairs={{0,16},{8,24},{16,0},{24,8},{1,17},{9,25},{17,1},{25,9},{2,18},{10... | collective-permute-start | bytes 393224 | tf_op jit(solution)/shard_map/ppermute | solution.py:476
  5.6 1.7 %copy-start.10 = (bf16[128,512]{1,0:T(8,128)(2,1)S(1)}, bf16[128,512]{1,0:T(8,128)(2,1)}, u32[]{:S(2)}) copy-start(bf16[128,512]{1,0:T(8,128)(2,1)} %refs_0_.1) | copy-start | bytes 393220
  5.6 2.3 %copy-start.3 = (bf16[512,16]{0,1:T(8,128)(2,1)S(1)}, bf16[512,16]{0,1:T(8,128)(2,1)}, u32[]{:S(2)}) copy-start(bf16[512,16]{0,1:T(8,128)(2,1)} %param.14) | copy-start | bytes 49156
  5.7 2.3 %copy-start.6 = (f32[512]{0:T(512)S(1)}, f32[512]{0:T(512)}, u32[]{:S(2)}) copy-start(f32[512]{0:T(512)} %param.12) | copy-start | bytes 6148
  5.7 2.3 %copy-start.7 = (f32[16]{0:T(128)S(1)}, f32[16]{0:T(128)}, u32[]{:S(2)}) copy-start(f32[16]{0:T(128)} %param.17) | copy-start | bytes 196
  5.7 2.3 %copy-start.8 = (f32[16]{0:T(128)S(1)}, f32[16]{0:T(128)}, u32[]{:S(2)}) copy-start(f32[16]{0:T(128)} %param.18) | copy-start | bytes 196
  7.3 1.7 %copy-start.1 = (bf16[1024,512]{1,0:T(8,128)(2,1)S(1)}, bf16[1024,512]{1,0:T(8,128)(2,1)}, u32[]{:S(2)}) copy-start(bf16[1024,512]{1,0:T(8,128)(2,1)} %refs_11_.1) | copy-start | bytes 3145732
  7.3 1.7 %copy-start.5 = (f32[1024]{0:T(1024)S(1)}, f32[1024]{0:T(1024)}, u32[]{:S(2)}) copy-start(f32[1024]{0:T(1024)} %param.20) | copy-start | bytes 12292
  7.4 1.7 %copy-start.9 = (f32[16]{0:T(128)S(1)}, f32[16]{0:T(128)}, u32[]{:S(2)}) copy-start(f32[16]{0:T(128)} %param.19) | copy-start | bytes 196
  7.4 1.6 %collective-permute-start.1 = (bf16[128,512]{1,0:T(8,128)(2,1)S(1)}, bf16[128,512]{1,0:T(8,128)(2,1)S(1)}, u32[]{:S(2)}, u32[]{:S(2)}) collective-permute-start(bf16[128,512]{1,0:T(8,128)(2,1)S(1)} %copy-done.10), channel_id=1, source_target_pairs={{0,8},{8,0},{16,24},{24,16},{1,9},{9,1},{17,25},{25,17},{2,10},{10... | collective-permute-start | bytes 393224 | tf_op jit(solution)/shard_map/ppermute | solution.py:476
  7.5 1.6 %collective-permute-start.2 = (bf16[128,512]{1,0:T(8,128)(2,1)S(1)}, bf16[128,512]{1,0:T(8,128)(2,1)S(1)}, u32[]{:S(2)}, u32[]{:S(2)}) collective-permute-start(bf16[128,512]{1,0:T(8,128)(2,1)S(1)} %collective-permute-done.block_ref), channel_id=1, source_target_pairs={{0,8},{8,0},{16,24},{24,16},{1,9},{9,1},{17,25},{25,17},{2,10},{10... | collective-permute-start | bytes 393224 | tf_op jit(solution)/shard_map/ppermute | solution.py:476

commit v3 on v2

--- a/solution.py
+++ b/solution.py
@@ -19,6 +19,7 @@
 GROUPS = EMBED // 128
 PAD = 8
 EDGE = 16
+UPFRONT = 4
 eps = 1e-05
 F32 = jnp.float32
 BF16 = jnp.bfloat16
@@ -119,21 +120,21 @@
     return result
 
 
-def decay_kernel(*refs):
-    sources, refs = refs[:5], refs[5:]
-    (normal_ref, decay_ref, lift_ref), refs = refs[:3], refs[3:]
-    held, semaphores = refs[:5], refs[5]
+def own_kernel(*refs):
+    sources, refs = refs[:8], refs[8:]
+    (decay_ref, lift_ref, activated_ref, edge_ref, silu_gate_ref), refs = refs[:5], refs[5:]
+    held, (x_ref, extended_ref, semaphores) = refs[:7], refs[7:]
     copies = [
-        pltpu.make_async_copy(sources[place], held[place], semaphores.at[place])
-        for place in range(5)
+        pltpu.make_async_copy(source, target, semaphores.at[place])
+        for place, (source, target) in enumerate(zip(sources, (x_ref, *held)))
     ]
     for copy in copies:
         copy.start()
-    for copy in copies:
+    norm_gain_ref, step_weight_ref, step_bias_ref, log_rate_ref = held[:4]
+    input_weight_ref, conv_weight_ref, conv_bias_ref = held[4:]
+    for copy in copies[:5]:
         copy.wait()
-    x_ref, norm_gain_ref, step_weight_ref, step_bias_ref, log_rate_ref = held
     normal = jnp.concatenate(both_normed(x_ref[...], norm_gain_ref[...], reversal()), axis=0)
-    normal_ref[...] = normal
     log_decay = log_decays(
         dot_rows(step_weight_ref[...], normal), step_bias_ref[...], log_rate_ref[...]
     )
@@ -143,44 +144,44 @@
     before = exact_dot(both, (row <= column).astype(BF16))
     after = exact_dot(both, (row >= column).astype(BF16))
     twos, fours = selectors(3, 2), selectors(1, 4)
-    for flip in range(2):
-        heads = slice(flip * HEADS, (flip + 1) * HEADS)
-        ones = jnp.ones((3 * HEADS, BLOCK), BF16)
-        sides = []
-        for rows in (before, after):
-            parts = stacked_split(rows[heads], 3)
-            sides.append((jnp.concatenate([parts, ones], axis=0), jnp.concatenate([-parts] * 2, 1)))
-
-        def spread(side, pair):
-            plus, minus = sides[side]
-            return dot_columns(plus, jnp.concatenate([twos[pair], twos[pair] * minus], axis=0))
-
-        for pair in range(PAIRS):
-            from_start, to_end = spread(0, pair), spread(1, pair)
-            for near in range(2):
-                lanes = lanes_of(near)
-                decay_ref[flip, 2 * pair + near] = jnp.exp(
-                    jnp.where(lower, from_start[:, lanes], to_end[:, lanes])
-                ).astype(BF16)
-        for way, rows in enumerate((before, after)):
-            lifts = jnp.exp(rows[heads]).astype(BF16)
-            for place, (start, stop) in enumerate(chunks(E)):
-                lift_ref[2 * flip + way, :, start:stop] = dot_columns(lifts, fours[place]).astype(
-                    BF16
-                )
-
-
-def own_kernel(
-    normal_ref,
-    input_weight_ref,
-    conv_weight_ref,
-    conv_bias_ref,
-    activated_ref,
-    edge_ref,
-    silu_gate_ref,
-    extended_ref,
-):
-    normal = normal_ref[...]
+    ones = jnp.ones((3 * HEADS, BLOCK), BF16)
+
+    def sides_of(rows):
+        parts = stacked_split(rows, 3)
+        return jnp.concatenate([parts, ones], axis=0), jnp.concatenate([-parts] * 2, axis=1)
+
+    heads = [slice(flip * HEADS, (flip + 1) * HEADS) for flip in range(2)]
+    sides = [[sides_of(rows[heads[flip]]) for rows in (before, after)] for flip in range(2)]
+    lifts = [[jnp.exp(rows[heads[flip]]).astype(BF16) for rows in (before, after)] for flip in range(2)]
+
+    def put_decay(flip, pair):
+        spreads = [
+            dot_columns(plus, jnp.concatenate([twos[pair], twos[pair] * minus], axis=0))
+            for plus, minus in sides[flip]
+        ]
+        for near in range(2):
+            lanes = lanes_of(near)
+            decay_ref[flip, 2 * pair + near] = jnp.exp(
+                jnp.where(lower, spreads[0][:, lanes], spreads[1][:, lanes])
+            ).astype(BF16)
+
+    def put_lift(flip, way, place):
+        start, stop = chunks(E)[place]
+        lift_ref[2 * flip + way, :, start:stop] = dot_columns(
+            lifts[flip][way], fours[place]
+        ).astype(BF16)
+
+    spare = [functools.partial(put_decay, flip, pair) for flip in range(2) for pair in range(PAIRS)]
+    spare += [
+        functools.partial(put_lift, flip, way, place)
+        for flip in range(2)
+        for way in range(2)
+        for place in range(PAIRS // 2)
+    ]
+    for _ in range(UPFRONT):
+        spare.pop(0)()
+    for copy in copies[5:]:
+        copy.wait()
     taps, bias = 0.5 * conv_weight_ref[...], 0.5 * conv_bias_ref[...].reshape(1, MIXED)
     for start, stop in chunks(MIXED):
         mixed = dot(normal, input_weight_ref[:, E + start : E + stop])
@@ -194,14 +195,24 @@
                 place[:PAD] = jnp.zeros((PAD, 128), F32)
                 place[PAD + BLOCK :] = jnp.zeros((PAD, 128), F32)
                 place[PAD : PAD + BLOCK] = rows[:, tile * 128 - start : tile * 128 - start + 128]
+        for flip in range(2):
+            for tile in range(start // 128, stop // 128):
+                lanes = lanes_of(tile)
+                place = extended_ref.at[flip, tile]
                 for way in range(2):
+                    if spare:
+                        spare.pop(0)()
                     half = filtered(place, PAD, lanes, taps, bias, way == 1)
                     activated_ref[2 * flip + way, :, lanes] = half_silu(half).astype(BF16)
     for start, stop in chunks(E):
         gate = dot(normal, input_weight_ref[:, start:stop])
+        if spare:
+            spare.pop(0)()
         gate = half_silu(0.5 * gate)
         for flip in range(2):
             silu_gate_ref[flip, :, start:stop] = gate[flip * BLOCK : (flip + 1) * BLOCK]
+    for left_over in spare:
+        left_over()
 
 
 def chain_rows(mask, index, block, gain, swap):
@@ -512,37 +523,32 @@
             name=name,
         )(*operands)
 
-    small = (hidden, gain, step_map, step_bias, log_rate)
-    normal, decay, lift = call(
-        decay_kernel,
-        "decays",
-        [
-            shape((2 * BLOCK, EMBED), BF16),
-            shape((2, HEADS, BLOCK, BLOCK), BF16),
-            shape((4, BLOCK, E), BF16),
-        ],
-        [
-            *[pltpu.VMEM(part.shape, part.dtype) for part in small],
-            pltpu.SemaphoreType.DMA((5,)),
-        ],
-        [pltpu.with_memory_space_constraint(part, pltpu.HBM) for part in small],
-        10**9,
-        12,
-        pl.BlockSpec(memory_space=pltpu.HBM),
-    )
-    own = call(
+    operands = (
+        hidden, gain, step_map, step_bias, log_rate, input_weight, conv_weight, conv_bias
+    )
+    made = call(
         own_kernel,
         "own_rows",
         [
+            shape((2, HEADS, BLOCK, BLOCK), BF16),
+            shape((4, BLOCK, E), BF16),
             shape((4, BLOCK, MIXED), BF16),
             shape((2, 2 * EDGE, MIXED), F32),
             shape((2, BLOCK, E), F32),
+            *[shape(part.shape, part.dtype) for part in operands[1:]],
         ],
-        [pltpu.VMEM((2, TILES, BLOCK + 2 * PAD, 128), F32)],
-        [normal, input_weight, conv_weight, conv_bias],
-        10**9,
-        12,
-    )
+        [
+            pltpu.VMEM(hidden.shape, hidden.dtype),
+            pltpu.VMEM((2, TILES, BLOCK + 2 * PAD, 128), F32),
+            pltpu.SemaphoreType.DMA((8,)),
+        ],
+        [pltpu.with_memory_space_constraint(part, pltpu.HBM) for part in operands],
+        2 * 10**9,
+        24,
+        pl.BlockSpec(memory_space=pltpu.HBM),
+    )
+    decay, lift, *own = made[:5]
+    gain, step_map, step_bias, log_rate, input_weight, conv_weight, conv_bias = made[5:]
     start, across, decay, lift, *own = lax.optimization_barrier(
         (hidden, across, decay, lift, *own)
     )

time: 15.2 us -> 14.9 us (0.980)
    pallas_call x4 -> x3, Pallas kernels: 11.2 us -> 11.1 us  [call(): pl.pallas_call(kernel, out_shape=outs, in_specs=[spec] * len(operands), o...]
where the time goes in v3:
time: 14.9 us; the launch traced here: 14.7 us
  Pallas kernels  11.1 us (74%)
  starting transfers between devices  3.51 us (24%)
    pallas_call x3, Pallas kernels, call(): pl.pallas_call(kernel, out_shape=outs, in_specs=[spec] * len(operands), o...  11.1 us
    ppermute x3, starting transfers between devices, swapped(): return lax.ppermute(rows, 'seq', [(i, i ^ step) for i in range(count)])  3.51 us
  transfers between devices with their start and end apart: 3, of which 0 were waited for; matrix products, arithmetic and copies ran while one was open for 0% of the time, Pallas kernels for 35%

profile of v3, /device:TPU:0, one launch (start us, length us, event | category | flops | bytes accessed | tf_op | source)
XLA Modules:
  0.0 14.7 jit_solution(15142631989600165734)
XLA Ops:
  0.0 2.9 %collective-permute-start = (bf16[128,512]{1,0:T(8,128)(2,1)}, bf16[128,512]{1,0:T(8,128)(2,1)S(1)}, u32[]{:S(2)}, u32[]{:S(2)}) collective-permute-start(bf16[128,512]{1,0:T(8,128)(2,1)} %refs_0_.1), channel_id=1, source_target_pairs={{0,16},{8,24},{16,0},{24,8},{1,17},{9,25},{17,1},{25,9},{2,18},{10... | collective-permute-start | bytes 393224 | tf_op jit(solution)/shard_map/ppermute | solution.py:487
  2.9 0.0 copy-start.3
  2.9 4.2 %own_rows.1 = (bf16[2,16,128,128]{3,2,1,0:T(8,128)(2,1)S(1)}, bf16[4,128,1024]{2,1,0:T(8,128)(2,1)S(1)}, bf16[4,128,1152]{2,1,0:T(8,128)(2,1)S(1)}, f32[2,32,115...) custom-call(bf16[128,512]{1,0:T(8,128)(2,1)} %refs_0_.1, ...), custom_call_target="tpu_custom_call" | custom-call | flops 2000000000 | bytes 10000000 | tf_op jit(solution)/shard_map/own_rows/pallas_call | solution.py:513
  7.1 0.0 copy-start
  7.1 0.0 copy-start.1
  7.1 0.0 copy-start.2
  7.2 0.0 collective-permute-done.block_ref
  7.2 0.0 copy-done.3
  7.2 0.1 collective-permute-start.1
  7.3 0.5 %collective-permute-start.2 = (bf16[128,512]{1,0:T(8,128)(2,1)S(1)}, bf16[128,512]{1,0:T(8,128)(2,1)S(1)}, u32[]{:S(2)}, u32[]{:S(2)}) collective-permute-start(bf16[128,512]{1,0:T(8,128)(2,1)S(1)} %collective-permute-done.block_ref), channel_id=1, source_target_pairs={{0,8},{8,0},{16,24},{24,16},{1,9},{9,1},{17,25},{25,17},{2,10},{10... | collective-permute-start | bytes 393224 | tf_op jit(solution)/shard_map/ppermute | solution.py:487
  7.8 1.0 %across_rows.1 = (bf16[2,128,1152]{2,1,0:T(8,128)(2,1)S(1)}, f32[2,24,1152]{2,1,0:T(8,128)S(1)}, f32[16,256]{1,0:T(8,128)S(1)}) custom-call(bf16[128,512]{1,0:T(8,128)(2,1)S(1)} %collective-permute-done.block_ref, f32[1,512]{1,0:T(1,128)S(1)} %get-tuple-element.34.norm_gain_ref.refs_2_, bf16[512,2176]{1,0:T(8,128)(2,1)S(1)} %get-tuple-element.35.input_weight_ref.refs_3_, ...), custom_call_target="tpu_custom_call" | custom-call | flops 1000000000 | bytes 10000000 | tf_op jit(solution)/shard_map/across_rows/pallas_call | solution.py:513
  8.8 0.0 collective-permute-done.1.refs_0_
  8.8 0.0 collective-permute-done.2.refs_1_
  8.8 0.0 copy-done
  8.8 0.0 copy-done.1
  8.8 0.0 copy-done.2
  8.8 5.9 %join_blocks.1 = bf16[128,512]{1,0:T(8,128)(2,1)} custom-call(bf16[128,512]{1,0:T(8,128)(2,1)S(1)} %collective-permute-done.1.refs_0_, bf16[128,512]{1,0:T(8,128)(2,1)S(1)} %collective-permute-done.2.refs_1_, f32[1,512]{1,0:T(1,128)S(1)} %get-tuple-element.34.norm_gain_ref.refs_2_, bf16[512,2176]{1,0:T(8,128)(2,1)S(1)} %get-tuple-element.35.input_weight_ref.refs_3_, ...), custom_call_target="tpu_custom_call" | custom-call | flops 2000000000 | bytes 10000000 | tf_op jit(solution)/shard_map/join_blocks/pallas_call | solution.py:513
Async XLA Ops:
  0.0 7.2 %collective-permute-start = (bf16[128,512]{1,0:T(8,128)(2,1)}, bf16[128,512]{1,0:T(8,128)(2,1)S(1)}, u32[]{:S(2)}, u32[]{:S(2)}) collective-permute-start(bf16[128,512]{1,0:T(8,128)(2,1)} %refs_0_.1), channel_id=1, source_target_pairs={{0,16},{8,24},{16,0},{24,8},{1,17},{9,25},{17,1},{25,9},{2,18},{10... | collective-permute-start | bytes 393224 | tf_op jit(solution)/shard_map/ppermute | solution.py:487
  2.9 4.2 %copy-start.3 = (bf16[128,512]{1,0:T(8,128)(2,1)S(1)}, bf16[128,512]{1,0:T(8,128)(2,1)}, u32[]{:S(2)}) copy-start(bf16[128,512]{1,0:T(8,128)(2,1)} %refs_0_.1) | copy-start | bytes 393220
  7.1 1.7 %copy-start = (bf16[1024,512]{1,0:T(8,128)(2,1)S(1)}, bf16[1024,512]{1,0:T(8,128)(2,1)}, u32[]{:S(2)}) copy-start(bf16[1024,512]{1,0:T(8,128)(2,1)} %refs_11_.1) | copy-start | bytes 3145732
  7.1 1.7 %copy-start.1 = (f32[1024]{0:T(1024)S(1)}, f32[1024]{0:T(1024)}, u32[]{:S(2)}) copy-start(f32[1024]{0:T(1024)} %param.20) | copy-start | bytes 12292
  7.1 1.7 %copy-start.2 = (f32[16]{0:T(128)S(1)}, f32[16]{0:T(128)}, u32[]{:S(2)}) copy-start(f32[16]{0:T(128)} %param.19) | copy-start | bytes 196
  7.2 1.6 %collective-permute-start.1 = (bf16[128,512]{1,0:T(8,128)(2,1)S(1)}, bf16[128,512]{1,0:T(8,128)(2,1)S(1)}, u32[]{:S(2)}, u32[]{:S(2)}) collective-permute-start(bf16[128,512]{1,0:T(8,128)(2,1)S(1)} %copy-done.3), channel_id=1, source_target_pairs={{0,8},{8,0},{16,24},{24,16},{1,9},{9,1},{17,25},{25,17},{2,10},{10... | collective-permute-start | bytes 393224 | tf_op jit(solution)/shard_map/ppermute | solution.py:487
  7.3 1.5 %collective-permute-start.2 = (bf16[128,512]{1,0:T(8,128)(2,1)S(1)}, bf16[128,512]{1,0:T(8,128)(2,1)S(1)}, u32[]{:S(2)}, u32[]{:S(2)}) collective-permute-start(bf16[128,512]{1,0:T(8,128)(2,1)S(1)} %collective-permute-done.block_ref), channel_id=1, source_target_pairs={{0,8},{8,0},{16,24},{24,16},{1,9},{9,1},{17,25},{25,17},{2,10},{10... | collective-permute-start | bytes 393224 | tf_op jit(solution)/shard_map/ppermute | solution.py:487

commit v4 on v3

--- a/solution.py
+++ b/solution.py
@@ -120,20 +120,23 @@
     return result
 
 
-def own_kernel(*refs):
-    sources, refs = refs[:8], refs[8:]
-    (decay_ref, lift_ref, activated_ref, edge_ref, silu_gate_ref), refs = refs[:5], refs[5:]
-    held, (x_ref, extended_ref, semaphores) = refs[:7], refs[7:]
-    copies = [
-        pltpu.make_async_copy(source, target, semaphores.at[place])
-        for place, (source, target) in enumerate(zip(sources, (x_ref, *held)))
-    ]
-    for copy in copies:
-        copy.start()
-    norm_gain_ref, step_weight_ref, step_bias_ref, log_rate_ref = held[:4]
-    input_weight_ref, conv_weight_ref, conv_bias_ref = held[4:]
-    for copy in copies[:5]:
-        copy.wait()
+def own_kernel(
+    opening_ref,
+    x_ref,
+    norm_gain_ref,
+    step_weight_ref,
+    step_bias_ref,
+    log_rate_ref,
+    input_weight_ref,
+    conv_weight_ref,
+    conv_bias_ref,
+    decay_ref,
+    lift_ref,
+    activated_ref,
+    edge_ref,
+    silu_gate_ref,
+    extended_ref,
+):
     normal = jnp.concatenate(both_normed(x_ref[...], norm_gain_ref[...], reversal()), axis=0)
     log_decay = log_decays(
         dot_rows(step_weight_ref[...], normal), step_bias_ref[...], log_rate_ref[...]
@@ -180,8 +183,6 @@
     ]
     for _ in range(UPFRONT):
         spare.pop(0)()
-    for copy in copies[5:]:
-        copy.wait()
     taps, bias = 0.5 * conv_weight_ref[...], 0.5 * conv_bias_ref[...].reshape(1, MIXED)
     for start, stop in chunks(MIXED):
         mixed = dot(normal, input_weight_ref[:, E + start : E + stop])
@@ -508,6 +509,14 @@
     gain, step_map = row(norm_gain), step_weight.T
     step_bias, log_rate = row(step_bias), row(log_rate)
     across = swapped(hidden, top, count)
+    first = pl.pallas_call(
+        lambda out_ref: out_ref.__setitem__(..., jnp.zeros((8, 128), F32)),
+        out_shape=shape((8, 128), F32),
+        out_specs=whole,
+        compiler_params=pltpu.CompilerParams(vmem_limit_bytes=2**20),
+        cost_estimate=pl.CostEstimate(flops=8 * 10**9, bytes_accessed=10**6, transcendentals=0),
+        name="opening",
+    )()
 
     def call(kernel, name, outs, scratch, operands, flops, limit, spec=whole):
         return pl.pallas_call(
@@ -526,7 +535,7 @@
     operands = (
         hidden, gain, step_map, step_bias, log_rate, input_weight, conv_weight, conv_bias
     )
-    made = call(
+    decay, lift, *own = call(
         own_kernel,
         "own_rows",
         [
@@ -535,20 +544,12 @@
             shape((4, BLOCK, MIXED), BF16),
             shape((2, 2 * EDGE, MIXED), F32),
             shape((2, BLOCK, E), F32),
-            *[shape(part.shape, part.dtype) for part in operands[1:]],
         ],
-        [
-            pltpu.VMEM(hidden.shape, hidden.dtype),
-            pltpu.VMEM((2, TILES, BLOCK + 2 * PAD, 128), F32),
-            pltpu.SemaphoreType.DMA((8,)),
-        ],
-        [pltpu.with_memory_space_constraint(part, pltpu.HBM) for part in operands],
+        [pltpu.VMEM((2, TILES, BLOCK + 2 * PAD, 128), F32)],
+        [first, *operands],
         2 * 10**9,
-        24,
-        pl.BlockSpec(memory_space=pltpu.HBM),
-    )
-    decay, lift, *own = made[:5]
-    gain, step_map, step_bias, log_rate, input_weight, conv_weight, conv_bias = made[5:]
+        16,
+    )
     start, across, decay, lift, *own = lax.optimization_barrier(
         (hidden, across, decay, lift, *own)
     )

time: 14.9 us -> 14.5 us (0.973)
  Pallas kernels: 11.1 us -> 9.87 us
  waiting for transfers between devices: 0.01 us -> 0.71 us
    pallas_call x3, Pallas kernels: 11.1 us -> 9.87 us  [call(): pl.pallas_call(kernel, out_shape=outs, in_specs=[spec] * len(operands), o...]
    ppermute x3, waiting for transfers between devices: 0.01 us -> 0.71 us  [swapped(): return lax.ppermute(rows, 'seq', [(i, i ^ step) for i in range(count)])]
  transfers between devices with their start and end apart: 3 -> 3, of which waited for: 0 -> 1; matrix products, arithmetic and copies ran while one was open for 0% -> 0% of each run, Pallas kernels for 35% -> 27%
where the time goes in v4:
time: 14.5 us; the launch traced here: 14.3 us
  Pallas kernels  9.87 us (68%)
  starting transfers between devices  3.53 us (24%)
  waiting for transfers between devices  0.71 us (5%)
  between operations  0.15 us (1%)
    pallas_call x3, Pallas kernels, call(): pl.pallas_call(kernel, out_shape=outs, in_specs=[spec] * len(operands), o...  9.87 us
    ppermute x3, starting transfers between devices, swapped(): return lax.ppermute(rows, 'seq', [(i, i ^ step) for i in range(count)])  3.53 us
    ppermute x3, waiting for transfers between devices, swapped(): return lax.ppermute(rows, 'seq', [(i, i ^ step) for i in range(count)])  0.71 us
  transfers between devices with their start and end apart: 3, of which 1 were waited for; matrix products, arithmetic and copies ran while one was open for 0% of the time, Pallas kernels for 27%

profile of v4, /device:TPU:0, one launch (start us, length us, event | category | flops | bytes accessed | tf_op | source)
XLA Modules:
  0.0 14.3 jit_solution(12309842073129673593)
XLA Ops:
  0.0 0.0 copy-start.10
  0.0 0.0 copy-start.4
  0.0 0.0 copy-start.2
  0.0 0.0 copy-start
  0.0 0.0 copy-start.8
  0.0 0.0 copy-start.7
  0.0 0.0 copy-start.3
  0.0 0.0 copy-start.6
  0.0 3.0 %collective-permute-start = (bf16[128,512]{1,0:T(8,128)(2,1)}, bf16[128,512]{1,0:T(8,128)(2,1)S(1)}, u32[]{:S(2)}, u32[]{:S(2)}) collective-permute-start(bf16[128,512]{1,0:T(8,128)(2,1)} %x_ref.1), channel_id=1, source_target_pairs={{0,16},{8,24},{16,0},{24,8},{1,17},{9,25},{17,1},{25,9},{2,18},{10... | collective-permute-start | bytes 393224 | tf_op jit(solution)/shard_map/ppermute | solution.py:488
  3.1 0.0 copy-done.10
  3.1 0.0 copy-done.4
  3.1 0.0 copy-done.2
  3.1 0.0 copy-done
  3.1 0.0 copy-done.8
  3.1 0.0 copy-done.7
  3.1 0.0 copy-done.3
  3.1 0.0 copy-done.6
  3.1 2.9 %own_rows.1 = (bf16[2,16,128,128]{3,2,1,0:T(8,128)(2,1)S(1)}, bf16[4,128,1024]{2,1,0:T(8,128)(2,1)S(1)}, bf16[4,128,1152]{2,1,0:T(8,128)(2,1)S(1)}, f32[2,32,1152]{2,1,0:T(8,128)S(1)}, f32[2,128,1024]{2,1,0:T(8,128)S(1)}) custom-call(f32[8,128]{1,0:T(8,128)S(1)} %opening.1.opening_ref, bf16[128,512]{1,0:T(8,128)(2,1)S(1)} %copy-done.10, ...), custom_call_target="tpu_custom_call" | custom-call | flops 2000000000 | bytes 10000000 | tf_op jit(solution)/shard_map/own_rows/pallas_call | solution.py:522
  6.0 0.0 copy-start.1
  6.0 0.0 copy-start.5
  6.1 0.0 copy-start.9
  6.1 0.7 %collective-permute-done.block_ref = bf16[128,512]{1,0:T(8,128)(2,1)S(1)} collective-permute-done((bf16[128,512]{1,0:T(8,128)(2,1)}, bf16[128,512]{1,0:T(8,128)(2,1)S(1)}, u32[]{:S(2)}, u32[]{:S(2)}) %collective-permute-start) | collective-permute-done | bytes 131104 | tf_op jit(solution)/shard_map/ppermute | solution.py:488
  6.8 0.0 collective-permute-start.1
  6.8 0.5 %collective-permute-start.2 = (bf16[128,512]{1,0:T(8,128)(2,1)S(1)}, bf16[128,512]{1,0:T(8,128)(2,1)S(1)}, u32[]{:S(2)}, u32[]{:S(2)}) collective-permute-start(bf16[128,512]{1,0:T(8,128)(2,1)S(1)} %collective-permute-done.block_ref), channel_id=1, source_target_pairs={{0,8},{8,0},{16,24},{24,16},{1,9},{9,1},{17,25},{25,17},{2,10},{10... | collective-permute-start | bytes 393224 | tf_op jit(solution)/shard_map/ppermute | solution.py:488
  7.3 1.0 %across_rows.1 = (bf16[2,128,1152]{2,1,0:T(8,128)(2,1)S(1)}, f32[2,24,1152]{2,1,0:T(8,128)S(1)}, f32[16,256]{1,0:T(8,128)S(1)}) custom-call(bf16[128,512]{1,0:T(8,128)(2,1)S(1)} %collective-permute-done.block_ref, f32[1,512]{1,0:T(1,128)S(1)} %bitcast.11, bf16[512,2176]{1,0:T(8,128)(2,1)S(1)} %copy-done, bf16[16,512]{1,0:T(8,128)(2,1)S(1)} %bitcast.7, ...), custom_call_target="tpu_custom_call" | custom-call | flops 1000000000 | bytes 10000000 | tf_op jit(solution)/shard_map/across_rows/pallas_call | solution.py:522
  8.3 0.0 collective-permute-done.1.refs_0_
  8.3 0.0 collective-permute-done.2.refs_1_
  8.3 0.0 copy-done.1
  8.3 0.0 copy-done.5
  8.4 0.0 copy-done.9
  8.4 5.9 %join_blocks.1 = bf16[128,512]{1,0:T(8,128)(2,1)} custom-call(bf16[128,512]{1,0:T(8,128)(2,1)S(1)} %collective-permute-done.1.refs_0_, bf16[128,512]{1,0:T(8,128)(2,1)S(1)} %collective-permute-done.2.refs_1_, f32[1,512]{1,0:T(1,128)S(1)} %bitcast.12, bf16[512,2176]{1,0:T(8,128)(2,1)S(1)} %copy-done, bf16[16,512]{1,0:T(8,128)(2,1)S(1)} %bitcast.8, ...), custom_call_target="tpu_custom_call" | custom-call | flops 2000000000 | bytes 10000000 | tf_op jit(solution)/shard_map/join_blocks/pallas_call | solution.py:522
  (1 shorter events, 0.0 us)
Async XLA Ops:
  0.0 3.1 %copy-start.10 = (bf16[128,512]{1,0:T(8,128)(2,1)S(1)}, bf16[128,512]{1,0:T(8,128)(2,1)}, u32[]{:S(2)}) copy-start(bf16[128,512]{1,0:T(8,128)(2,1)} %x_ref.1) | copy-start | bytes 393220
  0.0 3.1 %copy-start.4 = (f32[1152]{0:T(1024)S(1)}, f32[1152]{0:T(1024)}, u32[]{:S(2)}) copy-start(f32[1152]{0:T(1024)} %refs_6_.1) | copy-start | bytes 13828
  0.0 3.1 %copy-start.2 = (f32[4,1152]{1,0:T(4,128)S(1)}, f32[4,1152]{1,0:T(4,128)}, u32[]{:S(2)}) copy-start(f32[4,1152]{1,0:T(4,128)} %refs_5_.1) | copy-start | bytes 55300
  0.0 3.1 %copy-start = (bf16[512,2176]{1,0:T(8,128)(2,1)S(1)}, bf16[512,2176]{1,0:T(8,128)(2,1)}, u32[]{:S(2)}) copy-start(bf16[512,2176]{1,0:T(8,128)(2,1)} %refs_3_.1) | copy-start | bytes 6684676
  0.0 3.1 %copy-start.8 = (f32[16]{0:T(128)S(1)}, f32[16]{0:T(128)}, u32[]{:S(2)}) copy-start(f32[16]{0:T(128)} %param.18) | copy-start | bytes 196
  0.0 3.1 %copy-start.7 = (f32[16]{0:T(128)S(1)}, f32[16]{0:T(128)}, u32[]{:S(2)}) copy-start(f32[16]{0:T(128)} %param.17) | copy-start | bytes 196
  0.0 3.1 %copy-start.3 = (bf16[512,16]{0,1:T(8,128)(2,1)S(1)}, bf16[512,16]{0,1:T(8,128)(2,1)}, u32[]{:S(2)}) copy-start(bf16[512,16]{0,1:T(8,128)(2,1)} %param.14) | copy-start | bytes 49156
  0.0 3.1 %copy-start.6 = (f32[512]{0:T(512)S(1)}, f32[512]{0:T(512)}, u32[]{:S(2)}) copy-start(f32[512]{0:T(512)} %param.12) | copy-start | bytes 6148
  0.0 6.7 %collective-permute-start = (bf16[128,512]{1,0:T(8,128)(2,1)}, bf16[128,512]{1,0:T(8,128)(2,1)S(1)}, u32[]{:S(2)}, u32[]{:S(2)}) collective-permute-start(bf16[128,512]{1,0:T(8,128)(2,1)} %x_ref.1), channel_id=1, source_target_pairs={{0,16},{8,24},{16,0},{24,8},{1,17},{9,25},{17,1},{25,9},{2,18},{10... | collective-permute-start | bytes 393224 | tf_op jit(solution)/shard_map/ppermute | solution.py:488
  6.0 2.3 %copy-start.1 = (bf16[1024,512]{1,0:T(8,128)(2,1)S(1)}, bf16[1024,512]{1,0:T(8,128)(2,1)}, u32[]{:S(2)}) copy-start(bf16[1024,512]{1,0:T(8,128)(2,1)} %refs_11_.1) | copy-start | bytes 3145732
  6.0 2.3 %copy-start.5 = (f32[1024]{0:T(1024)S(1)}, f32[1024]{0:T(1024)}, u32[]{:S(2)}) copy-start(f32[1024]{0:T(1024)} %param.20) | copy-start | bytes 12292
  6.1 2.3 %copy-start.9 = (f32[16]{0:T(128)S(1)}, f32[16]{0:T(128)}, u32[]{:S(2)}) copy-start(f32[16]{0:T(128)} %param.19) | copy-start | bytes 196
  6.8 1.6 %collective-permute-start.1 = (bf16[128,512]{1,0:T(8,128)(2,1)S(1)}, bf16[128,512]{1,0:T(8,128)(2,1)S(1)}, u32[]{:S(2)}, u32[]{:S(2)}) collective-permute-start(bf16[128,512]{1,0:T(8,128)(2,1)S(1)} %copy-done.10), channel_id=1, source_target_pairs={{0,8},{8,0},{16,24},{24,16},{1,9},{9,1},{17,25},{25,17},{2,10},{10... | collective-permute-start | bytes 393224 | tf_op jit(solution)/shard_map/ppermute | solution.py:488
  6.8 1.6 %collective-permute-start.2 = (bf16[128,512]{1,0:T(8,128)(2,1)S(1)}, bf16[128,512]{1,0:T(8,128)(2,1)S(1)}, u32[]{:S(2)}, u32[]{:S(2)}) collective-permute-start(bf16[128,512]{1,0:T(8,128)(2,1)S(1)} %collective-permute-done.block_ref), channel_id=1, source_target_pairs={{0,8},{8,0},{16,24},{24,16},{1,9},{9,1},{17,25},{25,17},{2,10},{10... | collective-permute-start | bytes 393224 | tf_op jit(solution)/shard_map/ppermute | solution.py:488

commit v5 on v4

--- a/solution.py
+++ b/solution.py
@@ -260,8 +260,8 @@
                 activated_ref[flip, :, lanes] = half_silu(half).astype(BF16)
 
 
-def join_kernel(count, top, *refs):
-    others = [mask for mask in range(1, count) if mask != top]
+def join_kernel(count, early, *refs):
+    others = [mask for mask in range(1, count) if mask not in early]
     received, refs = refs[: len(others)], refs[len(others) :]
     (
         norm_gain_ref,
@@ -279,9 +279,7 @@
         activated_ref,
         edge_ref,
         silu_gate_ref,
-        ahead_ref,
-        ahead_edge_ref,
-        ahead_log_decay_ref,
+        *ahead_refs,
         out_ref,
         normal_ref,
         extended_ref,
@@ -290,6 +288,7 @@
         patch_ref,
         gated_ref,
     ) = refs
+    ahead = {mask: ahead_refs[3 * at : 3 * at + 3] for at, mask in enumerate(early)}
     index = lax.axis_index("seq")
     swap = reversal()
     row, column = iota((BLOCK, BLOCK), 0), iota((BLOCK, BLOCK), 1)
@@ -298,7 +297,7 @@
     taps, bias = 0.5 * conv_weight_ref[...], 0.5 * conv_bias_ref[...].reshape(1, MIXED)
 
     def picked(rows, block):
-        result = jnp.zeros((PAD, rows[top].shape[1]), F32)
+        result = jnp.zeros((PAD, rows[early[0]].shape[1]), F32)
         for mask, part in rows.items():
             result = jnp.where((index ^ mask) == block, part, result)
         return result
@@ -317,7 +316,8 @@
         for place, mask in enumerate(others):
             low = (2 * place + flip) * BLOCK
             pieces[mask, flip] = log_decay[:, low : low + BLOCK]
-        pieces[top, flip] = ahead_log_decay_ref[:, flip * BLOCK : (flip + 1) * BLOCK]
+        for mask in early:
+            pieces[mask, flip] = ahead[mask][2][:, flip * BLOCK : (flip + 1) * BLOCK]
     parts = [(mask, flip) for mask in range(1, count) for flip in range(2)]
     tails = exact_dot(
         jnp.concatenate([pieces[part] for part in parts], axis=0), (row > column).astype(BF16)
@@ -358,7 +358,8 @@
         else:
             fades = coming
         for flip in range(2):
-            acted, last = {}, {top: ahead_edge_ref[flip, EDGE:, start:stop]}
+            acted = {}
+            last = {mask: ahead[mask][1][flip, EDGE:, start:stop] for mask in early}
             for place, mask in enumerate(others):
                 low = (2 * place + flip) * BLOCK
                 last[mask] = mixed[low + BLOCK - PAD : low + BLOCK]
@@ -370,11 +371,12 @@
             for mask in range(1, count):
                 block = index ^ mask
                 halo = picked(last, jnp.where(block < index, block - 1, block + 1))
-                if mask == top:
+                if mask in ahead:
                     near = []
+                    ahead_ref, ahead_edge_ref, _ = ahead[mask]
                     for tile in range(start // 128, stop // 128):
                         lanes = lanes_of(tile)
-                        spot = patch_ref.at[flip, tile]
+                        spot = patch_ref.at[2 * early.index(mask) + flip, tile]
                         spot[:PAD] = halo[:, tile * 128 - start : tile * 128 - start + 128]
                         spot[PAD:] = ahead_edge_ref[flip, :EDGE, lanes]
                         half = filtered(spot, PAD, lanes, taps, bias, False, EDGE)
@@ -550,30 +552,37 @@
         2 * 10**9,
         16,
     )
-    start, across, decay, lift, *own = lax.optimization_barrier(
-        (hidden, across, decay, lift, *own)
-    )
-    received = {0: start, top: across}
+    shared = [gain, input_weight, step_map, conv_weight, conv_bias, step_bias, log_rate]
+
+    def ahead(mask, block):
+        return call(
+            functools.partial(ahead_kernel, mask),
+            "ahead_rows",
+            [
+                shape((2, BLOCK, MIXED), BF16),
+                shape((2, EDGE + PAD, MIXED), F32),
+                shape((HEADS, 2 * BLOCK), F32),
+            ],
+            [pltpu.VMEM((2, TILES, PAD + BLOCK, 128), F32)],
+            [block, *shared],
+            10**9,
+            12,
+        )
+
+    done, received = {}, {0: hidden}
+    if top > 1:
+        received[1] = swapped(hidden, 1, count)
+        done[1] = ahead(1, received[1])
+    across, decay, lift, own, done = lax.optimization_barrier((across, decay, lift, own, done))
+    received[top] = across
     for bit in reversed(range(top.bit_length() - 1)):
         for mask in sorted(received):
-            received[mask | 1 << bit] = swapped(received[mask], 1 << bit, count)
-    shared = [gain, input_weight, step_map, conv_weight, conv_bias, step_bias, log_rate]
-    ahead = call(
-        functools.partial(ahead_kernel, top),
-        "across_rows",
-        [
-            shape((2, BLOCK, MIXED), BF16),
-            shape((2, EDGE + PAD, MIXED), F32),
-            shape((HEADS, 2 * BLOCK), F32),
-        ],
-        [pltpu.VMEM((2, TILES, PAD + BLOCK, 128), F32)],
-        [across, *shared],
-        10**9,
-        12,
-    )
-    others = [mask for mask in range(1, count) if mask != top]
+            if not mask & ((2 << bit) - 1) and mask | 1 << bit not in received:
+                received[mask | 1 << bit] = swapped(received[mask], 1 << bit, count)
+    done[top] = ahead(top, across)
+    others = [mask for mask in range(1, count) if mask not in done]
     (out,) = call(
-        functools.partial(join_kernel, count, top),
+        functools.partial(join_kernel, count, sorted(done)),
         "join_blocks",
         [shape((BLOCK, EMBED), BF16)],
         [
@@ -581,7 +590,7 @@
             pltpu.VMEM((2 * len(others), TILES, PAD + BLOCK, 128), F32),
             pltpu.VMEM((4, 2 * N, E), BF16),
             pltpu.VMEM((4, PAD + EDGE, MIXED), F32),
-            pltpu.VMEM((2, TILES, PAD + EDGE, 128), F32),
+            pltpu.VMEM((2 * len(done), TILES, PAD + EDGE, 128), F32),
             pltpu.VMEM((4, BLOCK, E), F32),
         ],
         [
@@ -593,7 +602,7 @@
             decay,
             lift,
             *own,
-            *ahead,
+            *[part for mask in sorted(done) for part in done[mask]],
         ],
         2 * 10**9,
         18 + 2 * len(others),

time: 14.5 us -> 14.1 us (0.972)
  waiting for transfers between devices: 0.71 us -> 0.01 us
  Pallas kernels: 9.87 us -> 10.2 us
    ppermute x3, waiting for transfers between devices: 0.71 us -> 0.01 us  [swapped(): return lax.ppermute(rows, 'seq', [(i, i ^ step) for i in range(count)])]
    pallas_call x3 -> x4, Pallas kernels: 9.87 us -> 10.2 us  [call(): pl.pallas_call(kernel, out_shape=outs, in_specs=[spec] * len(operands), o...]
  transfers between devices with their start and end apart: 3 -> 3, of which waited for: 1 -> 0; matrix products, arithmetic and copies ran while one was open for 0% -> 0% of each run, Pallas kernels for 27% -> 34%
where the time goes in v5:
time: 14.1 us; the launch traced here: 14 us
  Pallas kernels  10.2 us (72%)
  starting transfers between devices  3.59 us (25%)
  between operations  0.18 us (1%)
    pallas_call x4, Pallas kernels, call(): pl.pallas_call(kernel, out_shape=outs, in_specs=[spec] * len(operands), o...  10.2 us
    ppermute x3, starting transfers between devices, swapped(): return lax.ppermute(rows, 'seq', [(i, i ^ step) for i in range(count)])  3.59 us
  transfers between devices with their start and end apart: 3, of which 0 were waited for; matrix products, arithmetic and copies ran while one was open for 0% of the time, Pallas kernels for 34%

profile of v5, /device:TPU:0, one launch (start us, length us, event | category | flops | bytes accessed | tf_op | source)
XLA Modules:
  0.0 14.0 jit_solution(7999356867924224463)
XLA Ops:
  0.0 0.0 copy-start.10
  0.0 0.0 copy-start.4
  0.0 0.0 copy-start.2
  0.0 0.0 copy-start
  0.0 0.0 copy-start.8
  0.0 0.0 copy-start.7
  0.0 0.0 copy-start.3
  0.0 0.0 copy-start.6
  0.0 3.0 %collective-permute-start = (bf16[128,512]{1,0:T(8,128)(2,1)}, bf16[128,512]{1,0:T(8,128)(2,1)S(1)}, u32[]{:S(2)}, u32[]{:S(2)}) collective-permute-start(bf16[128,512]{1,0:T(8,128)(2,1)} %x_ref.1), channel_id=1, source_target_pairs={{0,16},{8,24},{16,0},{24,8},{1,17},{9,25},{17,1},{25,9},{2,18},{10... | collective-permute-start | bytes 393224 | tf_op jit(solution)/shard_map/ppermute | solution.py:490
  3.1 0.0 collective-permute-start.1
  3.1 0.0 copy-done.10
  3.1 0.0 copy-done.4
  3.1 0.0 copy-done.2
  3.1 0.0 copy-done
  3.1 0.0 copy-done.8
  3.1 0.0 copy-done.7
  3.1 0.0 copy-done.3
  3.1 0.0 copy-done.6
  3.1 2.8 %own_rows.1 = (bf16[2,16,128,128]{3,2,1,0:T(8,128)(2,1)S(1)}, bf16[4,128,1024]{2,1,0:T(8,128)(2,1)S(1)}, bf16[4,128,1152]{2,1,0:T(8,128)(2,1)S(1)}, f32[2,32,1152]{2,1,0:T(8,128)S(1)}, f32[2,128,1024]{2,1,0:T(8,128)S(1)}) custom-call(f32[8,128]{1,0:T(8,128)S(1)} %opening.1.opening_ref, bf16[128,512]{1,0:T(8,128)(2,1)S(1)} %copy-done.10, ...), custom_call_target="tpu_custom_call" | custom-call | flops 2000000000 | bytes 10000000 | tf_op jit(solution)/shard_map/own_rows/pallas_call | solution.py:524
  5.9 0.0 collective-permute-done.1.block_ref
  5.9 1.0 %ahead_rows.2 = (bf16[2,128,1152]{2,1,0:T(8,128)(2,1)S(1)}, f32[2,24,1152]{2,1,0:T(8,128)S(1)}, f32[16,256]{1,0:T(8,128)S(1)}) custom-call(bf16[128,512]{1,0:T(8,128)(2,1)S(1)} %collective-permute-done.1.block_ref, f32[1,512]{1,0:T(1,128)S(1)} %bitcast.12, bf16[512,2176]{1,0:T(8,128)(2,1)S(1)} %copy-done, bf16[16,512]{1,0:T(8,128)(2,1)S(1)} %bitcast.7, ...), custom_call_target="tpu_custom_call" | custom-call | flops 1000000000 | bytes 10000000 | tf_op jit(solution)/shard_map/ahead_rows/pallas_call | solution.py:524
  7.0 0.0 copy-start.1
  7.0 0.0 copy-start.5
  7.0 0.0 copy-start.9
  7.0 0.0 collective-permute-done.block_ref
  7.0 0.6 %collective-permute-start.2 = (bf16[128,512]{1,0:T(8,128)(2,1)S(1)}, bf16[128,512]{1,0:T(8,128)(2,1)S(1)}, u32[]{:S(2)}, u32[]{:S(2)}) collective-permute-start(bf16[128,512]{1,0:T(8,128)(2,1)S(1)} %collective-permute-done.block_ref), channel_id=1, source_target_pairs={{0,8},{8,0},{16,24},{24,16},{1,9},{9,1},{17,25},{25,17},{2,10},{10... | collective-permute-start | bytes 393224 | tf_op jit(solution)/shard_map/ppermute | solution.py:490
  7.6 1.0 %ahead_rows.3 = (bf16[2,128,1152]{2,1,0:T(8,128)(2,1)S(1)}, f32[2,24,1152]{2,1,0:T(8,128)S(1)}, f32[16,256]{1,0:T(8,128)S(1)}) custom-call(bf16[128,512]{1,0:T(8,128)(2,1)S(1)} %collective-permute-done.block_ref, f32[1,512]{1,0:T(1,128)S(1)} %bitcast.13, bf16[512,2176]{1,0:T(8,128)(2,1)S(1)} %copy-done, bf16[16,512]{1,0:T(8,128)(2,1)S(1)} %bitcast.8, ...), custom_call_target="tpu_custom_call" | custom-call | flops 1000000000 | bytes 10000000 | tf_op jit(solution)/shard_map/ahead_rows/pallas_call | solution.py:524
  8.6 0.0 collective-permute-done.2.refs_0_
  8.6 0.0 copy-done.1
  8.6 0.0 copy-done.5
  8.6 0.0 copy-done.9
  8.6 5.4 %join_blocks.1 = bf16[128,512]{1,0:T(8,128)(2,1)} custom-call(bf16[128,512]{1,0:T(8,128)(2,1)S(1)} %collective-permute-done.2.refs_0_, f32[1,512]{1,0:T(1,128)S(1)} %bitcast.14, bf16[512,2176]{1,0:T(8,128)(2,1)S(1)} %copy-done, bf16[16,512]{1,0:T(8,128)(2,1)S(1)} %bitcast.9, f32[4,1152]{1,0:T(4,128)S(1)} %copy-done.2, f32[1152]{0:T(1024)S(1)} %copy-done.4, ...), custom_call_target="tpu_custom_call" | custom-call | flops 2000000000 | bytes 10000000 | tf_op jit(solution)/shard_map/join_blocks/pallas_call | solution.py:524
  (1 shorter events, 0.0 us)
Async XLA Ops:
  0.0 3.1 %copy-start.10 = (bf16[128,512]{1,0:T(8,128)(2,1)S(1)}, bf16[128,512]{1,0:T(8,128)(2,1)}, u32[]{:S(2)}) copy-start(bf16[128,512]{1,0:T(8,128)(2,1)} %x_ref.1) | copy-start | bytes 393220
  0.0 3.1 %copy-start.4 = (f32[1152]{0:T(1024)S(1)}, f32[1152]{0:T(1024)}, u32[]{:S(2)}) copy-start(f32[1152]{0:T(1024)} %refs_5_.1) | copy-start | bytes 13828
  0.0 3.1 %copy-start.2 = (f32[4,1152]{1,0:T(4,128)S(1)}, f32[4,1152]{1,0:T(4,128)}, u32[]{:S(2)}) copy-start(f32[4,1152]{1,0:T(4,128)} %refs_4_.1) | copy-start | bytes 55300
  0.0 3.1 %copy-start = (bf16[512,2176]{1,0:T(8,128)(2,1)S(1)}, bf16[512,2176]{1,0:T(8,128)(2,1)}, u32[]{:S(2)}) copy-start(bf16[512,2176]{1,0:T(8,128)(2,1)} %refs_2_.1) | copy-start | bytes 6684676
  0.0 3.1 %copy-start.8 = (f32[16]{0:T(128)S(1)}, f32[16]{0:T(128)}, u32[]{:S(2)}) copy-start(f32[16]{0:T(128)} %param.18) | copy-start | bytes 196
  0.0 3.1 %copy-start.7 = (f32[16]{0:T(128)S(1)}, f32[16]{0:T(128)}, u32[]{:S(2)}) copy-start(f32[16]{0:T(128)} %param.17) | copy-start | bytes 196
  0.0 3.1 %copy-start.3 = (bf16[512,16]{0,1:T(8,128)(2,1)S(1)}, bf16[512,16]{0,1:T(8,128)(2,1)}, u32[]{:S(2)}) copy-start(bf16[512,16]{0,1:T(8,128)(2,1)} %param.14) | copy-start | bytes 49156
  0.0 3.1 %copy-start.6 = (f32[512]{0:T(512)S(1)}, f32[512]{0:T(512)}, u32[]{:S(2)}) copy-start(f32[512]{0:T(512)} %param.12) | copy-start | bytes 6148
  0.0 6.9 %collective-permute-start = (bf16[128,512]{1,0:T(8,128)(2,1)}, bf16[128,512]{1,0:T(8,128)(2,1)S(1)}, u32[]{:S(2)}, u32[]{:S(2)}) collective-permute-start(bf16[128,512]{1,0:T(8,128)(2,1)} %x_ref.1), channel_id=1, source_target_pairs={{0,16},{8,24},{16,0},{24,8},{1,17},{9,25},{17,1},{25,9},{2,18},{10... | collective-permute-start | bytes 393224 | tf_op jit(solution)/shard_map/ppermute | solution.py:490
  3.1 2.9 %collective-permute-start.1 = (bf16[128,512]{1,0:T(8,128)(2,1)}, bf16[128,512]{1,0:T(8,128)(2,1)S(1)}, u32[]{:S(2)}, u32[]{:S(2)}) collective-permute-start(bf16[128,512]{1,0:T(8,128)(2,1)} %x_ref.1), channel_id=1, source_target_pairs={{0,8},{8,0},{16,24},{24,16},{1,9},{9,1},{17,25},{25,17},{2,10},{10... | collective-permute-start | bytes 393224 | tf_op jit(solution)/shard_map/ppermute | solution.py:490
  7.0 1.6 %copy-start.1 = (bf16[1024,512]{1,0:T(8,128)(2,1)S(1)}, bf16[1024,512]{1,0:T(8,128)(2,1)}, u32[]{:S(2)}) copy-start(bf16[1024,512]{1,0:T(8,128)(2,1)} %refs_10_.1) | copy-start | bytes 3145732
  7.0 1.6 %copy-start.5 = (f32[1024]{0:T(1024)S(1)}, f32[1024]{0:T(1024)}, u32[]{:S(2)}) copy-start(f32[1024]{0:T(1024)} %param.20) | copy-start | bytes 12292
  7.0 1.6 %copy-start.9 = (f32[16]{0:T(128)S(1)}, f32[16]{0:T(128)}, u32[]{:S(2)}) copy-start(f32[16]{0:T(128)} %param.19) | copy-start | bytes 196
  7.0 1.6 %collective-permute-start.2 = (bf16[128,512]{1,0:T(8,128)(2,1)S(1)}, bf16[128,512]{1,0:T(8,128)(2,1)S(1)}, u32[]{:S(2)}, u32[]{:S(2)}) collective-permute-start(bf16[128,512]{1,0:T(8,128)(2,1)S(1)} %collective-permute-done.block_ref), channel_id=1, source_target_pairs={{0,8},{8,0},{16,24},{24,16},{1,9},{9,1},{17,25},{25,17},{2,10},{10... | collective-permute-start | bytes 393224 | tf_op jit(solution)/shard_map/ppermute | solution.py:490

commit v6 on v5

--- a/solution.py
+++ b/solution.py
@@ -19,7 +19,7 @@
 GROUPS = EMBED // 128
 PAD = 8
 EDGE = 16
-UPFRONT = 4
+UPFRONT = 0
 eps = 1e-05
 F32 = jnp.float32
 BF16 = jnp.bfloat16
@@ -184,8 +184,12 @@
     for _ in range(UPFRONT):
         spare.pop(0)()
     taps, bias = 0.5 * conv_weight_ref[...], 0.5 * conv_bias_ref[...].reshape(1, MIXED)
-    for start, stop in chunks(MIXED):
-        mixed = dot(normal, input_weight_ref[:, E + start : E + stop])
+    order = chunks(MIXED)
+    ready = dot(normal, input_weight_ref[:, E : E + order[0][1]])
+    for turn, (start, stop) in enumerate(order):
+        mixed = ready
+        if turn + 1 < len(order):
+            ready = dot(normal, input_weight_ref[:, E + stop : E + order[turn + 1][1]])
         for flip in range(2):
             rows = mixed[flip * BLOCK : (flip + 1) * BLOCK]
             edge_ref[flip, :EDGE, start:stop] = rows[:EDGE]
@@ -245,8 +249,12 @@
         dot_rows(step_weight_ref[...], normal), step_bias_ref[...], log_rate_ref[...]
     )
     taps, bias = 0.5 * conv_weight_ref[...], 0.5 * conv_bias_ref[...].reshape(1, MIXED)
-    for start, stop in chunks(MIXED):
-        mixed = dot(normal, input_weight_ref[:, E + start : E + stop])
+    order = chunks(MIXED)
+    ready = dot(normal, input_weight_ref[:, E : E + order[0][1]])
+    for turn, (start, stop) in enumerate(order):
+        mixed = ready
+        if turn + 1 < len(order):
+            ready = dot(normal, input_weight_ref[:, E + stop : E + order[turn + 1][1]])
         for flip in range(2):
             rows = mixed[flip * BLOCK : (flip + 1) * BLOCK]
             edge_ref[flip, :EDGE, start:stop] = rows[:EDGE]

time: 14.1 us -> 13.9 us (0.986)
  Pallas kernels: 10.2 us -> 9.97 us
    pallas_call x4, Pallas kernels: 10.2 us -> 9.97 us  [call(): pl.pallas_call(kernel, out_shape=outs, in_specs=[spec] * len(operands), o...]
  transfers between devices with their start and end apart: 3 -> 3, of which waited for: 0 -> 0; matrix products, arithmetic and copies ran while one was open for 0% -> 0% of each run, Pallas kernels for 34% -> 33%
where the time goes in v6:
time: 13.9 us; the launch traced here: 13.8 us
  Pallas kernels  9.97 us (72%)
  starting transfers between devices  3.58 us (26%)
  between operations  0.18 us (1%)
    pallas_call x4, Pallas kernels, call(): pl.pallas_call(kernel, out_shape=outs, in_specs=[spec] * len(operands), o...  9.97 us
    ppermute x3, starting transfers between devices, swapped(): return lax.ppermute(rows, 'seq', [(i, i ^ step) for i in range(count)])  3.58 us
  transfers between devices with their start and end apart: 3, of which 0 were waited for; matrix products, arithmetic and copies ran while one was open for 0% of the time, Pallas kernels for 33%

profile of v6, /device:TPU:0, one launch (start us, length us, event | category | flops | bytes accessed | tf_op | source)
XLA Modules:
  0.0 13.8 jit_solution(14528630718892443115)
XLA Ops:
  0.0 0.0 copy-start.10
  0.0 0.0 copy-start.4
  0.0 0.0 copy-start.2
  0.0 0.0 copy-start
  0.0 0.0 copy-start.8
  0.0 0.0 copy-start.7
  0.0 0.0 copy-start.3
  0.0 0.0 copy-start.6
  0.0 3.0 %collective-permute-start = (bf16[128,512]{1,0:T(8,128)(2,1)}, bf16[128,512]{1,0:T(8,128)(2,1)S(1)}, u32[]{:S(2)}, u32[]{:S(2)}) collective-permute-start(bf16[128,512]{1,0:T(8,128)(2,1)} %x_ref.1), channel_id=1, source_target_pairs={{0,16},{8,24},{16,0},{24,8},{1,17},{9,25},{17,1},{25,9},{2,18},{10... | collective-permute-start | bytes 393224 | tf_op jit(solution)/shard_map/ppermute | solution.py:498
  3.1 0.0 collective-permute-start.1
  3.1 0.0 copy-done.10
  3.1 0.0 copy-done.4
  3.1 0.0 copy-done.2
  3.1 0.0 copy-done
  3.1 0.0 copy-done.8
  3.1 0.0 copy-done.7
  3.1 0.0 copy-done.3
  3.1 0.0 copy-done.6
  3.1 2.6 %own_rows.1 = (bf16[2,16,128,128]{3,2,1,0:T(8,128)(2,1)S(1)}, bf16[4,128,1024]{2,1,0:T(8,128)(2,1)S(1)}, bf16[4,128,1152]{2,1,0:T(8,128)(2,1)S(1)}, f32[2,32,1152]{2,1,0:T(8,128)S(1)}, f32[2,128,1024]{2,1,0:T(8,128)S(1)}) custom-call(f32[8,128]{1,0:T(8,128)S(1)} %opening.1.opening_ref, bf16[128,512]{1,0:T(8,128)(2,1)S(1)} %copy-done.10, ...), custom_call_target="tpu_custom_call" | custom-call | flops 2000000000 | bytes 10000000 | tf_op jit(solution)/shard_map/own_rows/pallas_call | solution.py:532
  5.7 0.0 collective-permute-done.1.block_ref
  5.7 1.0 %ahead_rows.2 = (bf16[2,128,1152]{2,1,0:T(8,128)(2,1)S(1)}, f32[2,24,1152]{2,1,0:T(8,128)S(1)}, f32[16,256]{1,0:T(8,128)S(1)}) custom-call(bf16[128,512]{1,0:T(8,128)(2,1)S(1)} %collective-permute-done.1.block_ref, f32[1,512]{1,0:T(1,128)S(1)} %bitcast.12, bf16[512,2176]{1,0:T(8,128)(2,1)S(1)} %copy-done, bf16[16,512]{1,0:T(8,128)(2,1)S(1)} %bitcast.7, ...), custom_call_target="tpu_custom_call" | custom-call | flops 1000000000 | bytes 10000000 | tf_op jit(solution)/shard_map/ahead_rows/pallas_call | solution.py:532
  6.7 0.0 copy-start.1
  6.8 0.0 copy-start.5
  6.8 0.0 copy-start.9
  6.8 0.0 collective-permute-done.block_ref
  6.8 0.6 %collective-permute-start.2 = (bf16[128,512]{1,0:T(8,128)(2,1)S(1)}, bf16[128,512]{1,0:T(8,128)(2,1)S(1)}, u32[]{:S(2)}, u32[]{:S(2)}) collective-permute-start(bf16[128,512]{1,0:T(8,128)(2,1)S(1)} %collective-permute-done.block_ref), channel_id=1, source_target_pairs={{0,8},{8,0},{16,24},{24,16},{1,9},{9,1},{17,25},{25,17},{2,10},{10... | collective-permute-start | bytes 393224 | tf_op jit(solution)/shard_map/ppermute | solution.py:498
  7.4 1.0 %ahead_rows.3 = (bf16[2,128,1152]{2,1,0:T(8,128)(2,1)S(1)}, f32[2,24,1152]{2,1,0:T(8,128)S(1)}, f32[16,256]{1,0:T(8,128)S(1)}) custom-call(bf16[128,512]{1,0:T(8,128)(2,1)S(1)} %collective-permute-done.block_ref, f32[1,512]{1,0:T(1,128)S(1)} %bitcast.13, bf16[512,2176]{1,0:T(8,128)(2,1)S(1)} %copy-done, bf16[16,512]{1,0:T(8,128)(2,1)S(1)} %bitcast.8, ...), custom_call_target="tpu_custom_call" | custom-call | flops 1000000000 | bytes 10000000 | tf_op jit(solution)/shard_map/ahead_rows/pallas_call | solution.py:532
  8.4 0.0 collective-permute-done.2.refs_0_
  8.4 0.0 copy-done.1
  8.4 0.0 copy-done.5
  8.4 0.0 copy-done.9
  8.4 5.4 %join_blocks.1 = bf16[128,512]{1,0:T(8,128)(2,1)} custom-call(bf16[128,512]{1,0:T(8,128)(2,1)S(1)} %collective-permute-done.2.refs_0_, f32[1,512]{1,0:T(1,128)S(1)} %bitcast.14, bf16[512,2176]{1,0:T(8,128)(2,1)S(1)} %copy-done, bf16[16,512]{1,0:T(8,128)(2,1)S(1)} %bitcast.9, f32[4,1152]{1,0:T(4,128)S(1)} %copy-done.2, f32[1152]{0:T(1024)S(1)} %copy-done.4, ...), custom_call_target="tpu_custom_call" | custom-call | flops 2000000000 | bytes 10000000 | tf_op jit(solution)/shard_map/join_blocks/pallas_call | solution.py:532
  (1 shorter events, 0.0 us)
Async XLA Ops:
  0.0 3.1 %copy-start.10 = (bf16[128,512]{1,0:T(8,128)(2,1)S(1)}, bf16[128,512]{1,0:T(8,128)(2,1)}, u32[]{:S(2)}) copy-start(bf16[128,512]{1,0:T(8,128)(2,1)} %x_ref.1) | copy-start | bytes 393220
  0.0 3.1 %copy-start.4 = (f32[1152]{0:T(1024)S(1)}, f32[1152]{0:T(1024)}, u32[]{:S(2)}) copy-start(f32[1152]{0:T(1024)} %refs_5_.1) | copy-start | bytes 13828
  0.0 3.1 %copy-start.2 = (f32[4,1152]{1,0:T(4,128)S(1)}, f32[4,1152]{1,0:T(4,128)}, u32[]{:S(2)}) copy-start(f32[4,1152]{1,0:T(4,128)} %refs_4_.1) | copy-start | bytes 55300
  0.0 3.1 %copy-start = (bf16[512,2176]{1,0:T(8,128)(2,1)S(1)}, bf16[512,2176]{1,0:T(8,128)(2,1)}, u32[]{:S(2)}) copy-start(bf16[512,2176]{1,0:T(8,128)(2,1)} %refs_2_.1) | copy-start | bytes 6684676
  0.0 3.1 %copy-start.8 = (f32[16]{0:T(128)S(1)}, f32[16]{0:T(128)}, u32[]{:S(2)}) copy-start(f32[16]{0:T(128)} %param.18) | copy-start | bytes 196
  0.0 3.1 %copy-start.7 = (f32[16]{0:T(128)S(1)}, f32[16]{0:T(128)}, u32[]{:S(2)}) copy-start(f32[16]{0:T(128)} %param.17) | copy-start | bytes 196
  0.0 3.1 %copy-start.3 = (bf16[512,16]{0,1:T(8,128)(2,1)S(1)}, bf16[512,16]{0,1:T(8,128)(2,1)}, u32[]{:S(2)}) copy-start(bf16[512,16]{0,1:T(8,128)(2,1)} %param.14) | copy-start | bytes 49156
  0.0 3.1 %copy-start.6 = (f32[512]{0:T(512)S(1)}, f32[512]{0:T(512)}, u32[]{:S(2)}) copy-start(f32[512]{0:T(512)} %param.12) | copy-start | bytes 6148
  0.0 6.7 %collective-permute-start = (bf16[128,512]{1,0:T(8,128)(2,1)}, bf16[128,512]{1,0:T(8,128)(2,1)S(1)}, u32[]{:S(2)}, u32[]{:S(2)}) collective-permute-start(bf16[128,512]{1,0:T(8,128)(2,1)} %x_ref.1), channel_id=1, source_target_pairs={{0,16},{8,24},{16,0},{24,8},{1,17},{9,25},{17,1},{25,9},{2,18},{10... | collective-permute-start | bytes 393224 | tf_op jit(solution)/shard_map/ppermute | solution.py:498
  3.1 2.7 %collective-permute-start.1 = (bf16[128,512]{1,0:T(8,128)(2,1)}, bf16[128,512]{1,0:T(8,128)(2,1)S(1)}, u32[]{:S(2)}, u32[]{:S(2)}) collective-permute-start(bf16[128,512]{1,0:T(8,128)(2,1)} %x_ref.1), channel_id=1, source_target_pairs={{0,8},{8,0},{16,24},{24,16},{1,9},{9,1},{17,25},{25,17},{2,10},{10... | collective-permute-start | bytes 393224 | tf_op jit(solution)/shard_map/ppermute | solution.py:498
  6.7 1.6 %copy-start.1 = (bf16[1024,512]{1,0:T(8,128)(2,1)S(1)}, bf16[1024,512]{1,0:T(8,128)(2,1)}, u32[]{:S(2)}) copy-start(bf16[1024,512]{1,0:T(8,128)(2,1)} %refs_10_.1) | copy-start | bytes 3145732
  6.8 1.6 %copy-start.5 = (f32[1024]{0:T(1024)S(1)}, f32[1024]{0:T(1024)}, u32[]{:S(2)}) copy-start(f32[1024]{0:T(1024)} %param.20) | copy-start | bytes 12292
  6.8 1.6 %copy-start.9 = (f32[16]{0:T(128)S(1)}, f32[16]{0:T(128)}, u32[]{:S(2)}) copy-start(f32[16]{0:T(128)} %param.19) | copy-start | bytes 196
  6.8 1.6 %collective-permute-start.2 = (bf16[128,512]{1,0:T(8,128)(2,1)S(1)}, bf16[128,512]{1,0:T(8,128)(2,1)S(1)}, u32[]{:S(2)}, u32[]{:S(2)}) collective-permute-start(bf16[128,512]{1,0:T(8,128)(2,1)S(1)} %collective-permute-done.block_ref), channel_id=1, source_target_pairs={{0,8},{8,0},{16,24},{24,16},{1,9},{9,1},{17,25},{25,17},{2,10},{10... | collective-permute-start | bytes 393224 | tf_op jit(solution)/shard_map/ppermute | solution.py:498

commit v7 on v6

--- a/solution.py
+++ b/solution.py
@@ -209,10 +209,15 @@
                         spare.pop(0)()
                     half = filtered(place, PAD, lanes, taps, bias, way == 1)
                     activated_ref[2 * flip + way, :, lanes] = half_silu(half).astype(BF16)
-    for start, stop in chunks(E):
-        gate = dot(normal, input_weight_ref[:, start:stop])
-        if spare:
-            spare.pop(0)()
+    order = chunks(E)
+    ready = dot(normal, input_weight_ref[:, : order[0][1]])
+    for turn, (start, stop) in enumerate(order):
+        gate = ready
+        if turn + 1 < len(order):
+            ready = dot(normal, input_weight_ref[:, stop : order[turn + 1][1]])
+        for _ in range(2):
+            if spare:
+                spare.pop(0)()
         gate = half_silu(0.5 * gate)
         for flip in range(2):
             silu_gate_ref[flip, :, start:stop] = gate[flip * BLOCK : (flip + 1) * BLOCK]

time: 13.9 us -> 13.9 us (level)
  no operation moved by 1% of the time
where the time goes in v7:
time: 13.9 us; the launch traced here: 13.8 us
  Pallas kernels  9.97 us (72%)
  starting transfers between devices  3.58 us (26%)
  between operations  0.18 us (1%)
    pallas_call x4, Pallas kernels, call(): pl.pallas_call(kernel, out_shape=outs, in_specs=[spec] * len(operands), o...  9.97 us
    ppermute x3, starting transfers between devices, swapped(): return lax.ppermute(rows, 'seq', [(i, i ^ step) for i in range(count)])  3.58 us
  transfers between devices with their start and end apart: 3, of which 0 were waited for; matrix products, arithmetic and copies ran while one was open for 0% of the time, Pallas kernels for 33%

profile of v7, /device:TPU:0, one launch (start us, length us, event | category | flops | bytes accessed | tf_op | source)
XLA Modules:
  0.0 13.8 jit_solution(14528630718892443115)
XLA Ops:
  0.0 0.0 copy-start.10
  0.0 0.0 copy-start.4
  0.0 0.0 copy-start.2
  0.0 0.0 copy-start
  0.0 0.0 copy-start.8
  0.0 0.0 copy-start.7
  0.0 0.0 copy-start.3
  0.0 0.0 copy-start.6
  0.0 3.0 %collective-permute-start = (bf16[128,512]{1,0:T(8,128)(2,1)}, bf16[128,512]{1,0:T(8,128)(2,1)S(1)}, u32[]{:S(2)}, u32[]{:S(2)}) collective-permute-start(bf16[128,512]{1,0:T(8,128)(2,1)} %x_ref.1), channel_id=1, source_target_pairs={{0,16},{8,24},{16,0},{24,8},{1,17},{9,25},{17,1},{25,9},{2,18},{10... | collective-permute-start | bytes 393224 | tf_op jit(solution)/shard_map/ppermute | solution.py:503
  3.1 0.0 collective-permute-start.1
  3.1 0.0 copy-done.10
  3.1 0.0 copy-done.4
  3.1 0.0 copy-done.2
  3.1 0.0 copy-done
  3.1 0.0 copy-done.8
  3.1 0.0 copy-done.7
  3.1 0.0 copy-done.3
  3.1 0.0 copy-done.6
  3.1 2.6 %own_rows.1 = (bf16[2,16,128,128]{3,2,1,0:T(8,128)(2,1)S(1)}, bf16[4,128,1024]{2,1,0:T(8,128)(2,1)S(1)}, bf16[4,128,1152]{2,1,0:T(8,128)(2,1)S(1)}, f32[2,32,1152]{2,1,0:T(8,128)S(1)}, f32[2,128,1024]{2,1,0:T(8,128)S(1)}) custom-call(f32[8,128]{1,0:T(8,128)S(1)} %opening.1.opening_ref, bf16[128,512]{1,0:T(8,128)(2,1)S(1)} %copy-done.10, ...), custom_call_target="tpu_custom_call" | custom-call | flops 2000000000 | bytes 10000000 | tf_op jit(solution)/shard_map/own_rows/pallas_call | solution.py:537
  5.7 0.0 collective-permute-done.1.block_ref
  5.7 1.0 %ahead_rows.2 = (bf16[2,128,1152]{2,1,0:T(8,128)(2,1)S(1)}, f32[2,24,1152]{2,1,0:T(8,128)S(1)}, f32[16,256]{1,0:T(8,128)S(1)}) custom-call(bf16[128,512]{1,0:T(8,128)(2,1)S(1)} %collective-permute-done.1.block_ref, f32[1,512]{1,0:T(1,128)S(1)} %bitcast.12, bf16[512,2176]{1,0:T(8,128)(2,1)S(1)} %copy-done, bf16[16,512]{1,0:T(8,128)(2,1)S(1)} %bitcast.7, ...), custom_call_target="tpu_custom_call" | custom-call | flops 1000000000 | bytes 10000000 | tf_op jit(solution)/shard_map/ahead_rows/pallas_call | solution.py:537
  6.7 0.0 copy-start.1
  6.8 0.0 copy-start.5
  6.8 0.0 copy-start.9
  6.8 0.0 collective-permute-done.block_ref
  6.8 0.6 %collective-permute-start.2 = (bf16[128,512]{1,0:T(8,128)(2,1)S(1)}, bf16[128,512]{1,0:T(8,128)(2,1)S(1)}, u32[]{:S(2)}, u32[]{:S(2)}) collective-permute-start(bf16[128,512]{1,0:T(8,128)(2,1)S(1)} %collective-permute-done.block_ref), channel_id=1, source_target_pairs={{0,8},{8,0},{16,24},{24,16},{1,9},{9,1},{17,25},{25,17},{2,10},{10... | collective-permute-start | bytes 393224 | tf_op jit(solution)/shard_map/ppermute | solution.py:503
  7.4 1.0 %ahead_rows.3 = (bf16[2,128,1152]{2,1,0:T(8,128)(2,1)S(1)}, f32[2,24,1152]{2,1,0:T(8,128)S(1)}, f32[16,256]{1,0:T(8,128)S(1)}) custom-call(bf16[128,512]{1,0:T(8,128)(2,1)S(1)} %collective-permute-done.block_ref, f32[1,512]{1,0:T(1,128)S(1)} %bitcast.13, bf16[512,2176]{1,0:T(8,128)(2,1)S(1)} %copy-done, bf16[16,512]{1,0:T(8,128)(2,1)S(1)} %bitcast.8, ...), custom_call_target="tpu_custom_call" | custom-call | flops 1000000000 | bytes 10000000 | tf_op jit(solution)/shard_map/ahead_rows/pallas_call | solution.py:537
  8.4 0.0 collective-permute-done.2.refs_0_
  8.4 0.0 copy-done.1
  8.4 0.0 copy-done.5
  8.4 0.0 copy-done.9
  8.4 5.4 %join_blocks.1 = bf16[128,512]{1,0:T(8,128)(2,1)} custom-call(bf16[128,512]{1,0:T(8,128)(2,1)S(1)} %collective-permute-done.2.refs_0_, f32[1,512]{1,0:T(1,128)S(1)} %bitcast.14, bf16[512,2176]{1,0:T(8,128)(2,1)S(1)} %copy-done, bf16[16,512]{1,0:T(8,128)(2,1)S(1)} %bitcast.9, f32[4,1152]{1,0:T(4,128)S(1)} %copy-done.2, f32[1152]{0:T(1024)S(1)} %copy-done.4, ...), custom_call_target="tpu_custom_call" | custom-call | flops 2000000000 | bytes 10000000 | tf_op jit(solution)/shard_map/join_blocks/pallas_call | solution.py:537
  (1 shorter events, 0.0 us)
Async XLA Ops:
  0.0 3.1 %copy-start.10 = (bf16[128,512]{1,0:T(8,128)(2,1)S(1)}, bf16[128,512]{1,0:T(8,128)(2,1)}, u32[]{:S(2)}) copy-start(bf16[128,512]{1,0:T(8,128)(2,1)} %x_ref.1) | copy-start | bytes 393220
  0.0 3.1 %copy-start.4 = (f32[1152]{0:T(1024)S(1)}, f32[1152]{0:T(1024)}, u32[]{:S(2)}) copy-start(f32[1152]{0:T(1024)} %refs_5_.1) | copy-start | bytes 13828
  0.0 3.1 %copy-start.2 = (f32[4,1152]{1,0:T(4,128)S(1)}, f32[4,1152]{1,0:T(4,128)}, u32[]{:S(2)}) copy-start(f32[4,1152]{1,0:T(4,128)} %refs_4_.1) | copy-start | bytes 55300
  0.0 3.1 %copy-start = (bf16[512,2176]{1,0:T(8,128)(2,1)S(1)}, bf16[512,2176]{1,0:T(8,128)(2,1)}, u32[]{:S(2)}) copy-start(bf16[512,2176]{1,0:T(8,128)(2,1)} %refs_2_.1) | copy-start | bytes 6684676
  0.0 3.1 %copy-start.8 = (f32[16]{0:T(128)S(1)}, f32[16]{0:T(128)}, u32[]{:S(2)}) copy-start(f32[16]{0:T(128)} %param.18) | copy-start | bytes 196
  0.0 3.1 %copy-start.7 = (f32[16]{0:T(128)S(1)}, f32[16]{0:T(128)}, u32[]{:S(2)}) copy-start(f32[16]{0:T(128)} %param.17) | copy-start | bytes 196
  0.0 3.1 %copy-start.3 = (bf16[512,16]{0,1:T(8,128)(2,1)S(1)}, bf16[512,16]{0,1:T(8,128)(2,1)}, u32[]{:S(2)}) copy-start(bf16[512,16]{0,1:T(8,128)(2,1)} %param.14) | copy-start | bytes 49156
  0.0 3.1 %copy-start.6 = (f32[512]{0:T(512)S(1)}, f32[512]{0:T(512)}, u32[]{:S(2)}) copy-start(f32[512]{0:T(512)} %param.12) | copy-start | bytes 6148
  0.0 6.7 %collective-permute-start = (bf16[128,512]{1,0:T(8,128)(2,1)}, bf16[128,512]{1,0:T(8,128)(2,1)S(1)}, u32[]{:S(2)}, u32[]{:S(2)}) collective-permute-start(bf16[128,512]{1,0:T(8,128)(2,1)} %x_ref.1), channel_id=1, source_target_pairs={{0,16},{8,24},{16,0},{24,8},{1,17},{9,25},{17,1},{25,9},{2,18},{10... | collective-permute-start | bytes 393224 | tf_op jit(solution)/shard_map/ppermute | solution.py:503
  3.1 2.7 %collective-permute-start.1 = (bf16[128,512]{1,0:T(8,128)(2,1)}, bf16[128,512]{1,0:T(8,128)(2,1)S(1)}, u32[]{:S(2)}, u32[]{:S(2)}) collective-permute-start(bf16[128,512]{1,0:T(8,128)(2,1)} %x_ref.1), channel_id=1, source_target_pairs={{0,8},{8,0},{16,24},{24,16},{1,9},{9,1},{17,25},{25,17},{2,10},{10... | collective-permute-start | bytes 393224 | tf_op jit(solution)/shard_map/ppermute | solution.py:503
  6.7 1.6 %copy-start.1 = (bf16[1024,512]{1,0:T(8,128)(2,1)S(1)}, bf16[1024,512]{1,0:T(8,128)(2,1)}, u32[]{:S(2)}) copy-start(bf16[1024,512]{1,0:T(8,128)(2,1)} %refs_10_.1) | copy-start | bytes 3145732
  6.8 1.6 %copy-start.5 = (f32[1024]{0:T(1024)S(1)}, f32[1024]{0:T(1024)}, u32[]{:S(2)}) copy-start(f32[1024]{0:T(1024)} %param.20) | copy-start | bytes 12292
  6.8 1.6 %copy-start.9 = (f32[16]{0:T(128)S(1)}, f32[16]{0:T(128)}, u32[]{:S(2)}) copy-start(f32[16]{0:T(128)} %param.19) | copy-start | bytes 196
  6.8 1.6 %collective-permute-start.2 = (bf16[128,512]{1,0:T(8,128)(2,1)S(1)}, bf16[128,512]{1,0:T(8,128)(2,1)S(1)}, u32[]{:S(2)}, u32[]{:S(2)}) collective-permute-start(bf16[128,512]{1,0:T(8,128)(2,1)S(1)} %collective-permute-done.block_ref), channel_id=1, source_target_pairs={{0,8},{8,0},{16,24},{24,16},{1,9},{9,1},{17,25},{25,17},{2,10},{10... | collective-permute-start | bytes 393224 | tf_op jit(solution)/shard_map/ppermute | solution.py:503
